TPU v7x, 512 devices: a whole 4x8x8 slice. The times are simulated.
512 devices in a mesh: leaf: 128 (over y, z, core), coef: 4 (over x).
Axes of the slice: x: 4, y: 8, z: 8, core: 2. Of those that a mesh axis runs over, the one named last changes fastest.
Arguments:
- leaf_mult: bfloat16 [289, 524288], P(None, ('leaf', 'coef')), may hold values from -6 to 6
- fine_count: int32 [512], P(('leaf', 'coef')), may hold values from 256 to 1024, as said below
- parent_a: int32 [524288], P(('leaf', 'coef')), may hold values from 0 to 65535, as said below
- octant_a: int32 [524288], P(('leaf', 'coef')), may hold values from 0 to 7
- parent_b: int32 [65536], P(('leaf', 'coef')), may hold values from 0 to 8191, as said below
- octant_b: int32 [65536], P(('leaf', 'coef')), may hold values from 0 to 7
- parent_c: int32 [8192], P(('leaf', 'coef')), may hold values from 0 to 1023, as said below
- octant_c: int32 [8192], P(('leaf', 'coef')), may hold values from 0 to 7
- list_b_src: int32 [65536, 16], P(('leaf', 'coef')), may hold values from 0 to 65535, as said below
- list_b_off: int32 [65536, 16], P(('leaf', 'coef')), may hold values from 0 to 7
- list_t_src: int32 [1024, 16], replicated, may hold values from 0 to 1023
- list_t_off: int32 [1024, 16], replicated, may hold values from 0 to 7
- m2m_ops: bfloat16 [8, 289, 289], replicated, may hold values from -0.375 to 0.375
- m2l_ops: bfloat16 [8, 289, 289], replicated, may hold values from -0.375 to 0.375
Outputs:
- fine_local: bfloat16 [289, 524288], P(None, ('leaf', 'coef'))
Inputs may be any that keep to these rules, and one draw needn't show every extreme that they name: `fine_count`: the living fine cells of a device are the first ones of its range; some device is full and some holds a quarter of 1024. `parent_a`: the parent of a fine cell is a level-B cell of the same device; parents never fall along the cells. `parent_b`: the parent of a level-B cell is a level-C cell of the same device; parents never fall along the cells. `parent_c`: parents never fall along the cells; the children of a top cell may lie on several devices. `list_b_src`: every source lies on the target's device or on the device just before or just after it in order.
All inputs are finite; a program needn't handle non-finite values.
Results may differ from a plain program's by a relative error of at most 0.02.
Values may be sent and summed in bfloat16 or wider, within the bound.
A program may use at most 64 MiB of HBM per device.

v0:
```python
import jax
import jax.numpy as jnp
from jax import lax
from jax.sharding import PartitionSpec as P


def padded(shard, sides, width):
    for axis, dim in sides:
        size, length = (lax.axis_size(axis), shard.shape[dim])
        up = [(i, (i + 1) % size) for i in range(size - 1)]
        down = [(j, i) for i, j in up]
        last = lax.slice_in_dim(shard, length - width, length, axis=dim)
        leading = lax.slice_in_dim(shard, 0, width, axis=dim)
        before = lax.ppermute(last, axis, up)
        after = lax.ppermute(leading, axis, down)
        shard = jnp.concatenate([before, shard, after], axis=dim)
    return shard


def grouped_sum(expansion, slot_index, weight, segments):
    one_hot = (slot_index[:, None] == jnp.arange(8 * segments, dtype=jnp.int32)[None, :]) & weight[
        :, None
    ]
    summed = jnp.dot(expansion, one_hot.astype(jnp.bfloat16), preferred_element_type=jnp.float32)
    summed = summed.astype(jnp.bfloat16)
    return summed.reshape(expansion.shape[0], 8, segments).transpose(1, 0, 2)


def apply_stack(operators, stack):
    kinds, rows, inner = operators.shape
    joined_ops = operators.transpose(1, 0, 2).reshape(rows, kinds * inner)
    joined_stack = stack.reshape(kinds * inner, stack.shape[2])
    return jnp.dot(joined_ops, joined_stack, preferred_element_type=jnp.float32)


def per_cell(operators, source, octant):
    running = jnp.zeros(source.shape, jnp.float32)
    for which in range(8):
        shifted = jnp.dot(operators[which], source, preferred_element_type=jnp.float32)
        running = running + jnp.where(octant[None, :] == which, shifted, 0.0)
    return running


def descend(operators, source, parent, octant):
    width = source.shape[1]
    products = lax.dot_general(
        operators, source, (((1,), (0,)), ((), ())), preferred_element_type=jnp.float32
    )
    products = products.transpose(1, 0, 2).reshape(source.shape[0], 8 * width)
    return jnp.take(products, octant * width + parent, axis=1)


def pack(source, sources, offsets, offset_kinds):
    targets, entries = sources.shape
    gathered = jnp.take(source, sources.reshape(-1), axis=1).reshape(
        source.shape[0], targets, entries
    )
    one_hot = (
        offsets[:, :, None] == jnp.arange(offset_kinds, dtype=jnp.int32)[None, None, :]
    ).astype(jnp.bfloat16)
    packed = jnp.einsum("ktj,tjo->okt", gathered, one_hot, preferred_element_type=jnp.float32)
    return packed.astype(jnp.bfloat16)


def body(
    leaf_mult,
    fine_count,
    parent_a,
    octant_a,
    parent_b,
    octant_b,
    parent_c,
    octant_c,
    list_b_src,
    list_b_off,
    list_t_src,
    list_t_off,
    m2m_ops,
    m2l_ops,
):
    cells_a = leaf_mult.shape[1]
    cells_b = parent_b.shape[0]
    cells_c = parent_c.shape[0]
    top_cells = list_t_src.shape[0]
    offset_kinds = m2l_ops.shape[0]
    device = lax.axis_index(("leaf", "coef"))
    living = jnp.arange(cells_a, dtype=jnp.int32) < fine_count[0]
    local_parent_a = parent_a - device * cells_b
    local_parent_b = parent_b - device * cells_c
    grouped_b = grouped_sum(leaf_mult, octant_a * cells_b + local_parent_a, living, cells_b)
    mult_b = apply_stack(m2m_ops, grouped_b).astype(jnp.bfloat16)
    window = padded(mult_b, ((("leaf", "coef"), 1),), cells_b)
    near_b = apply_stack(
        m2l_ops, pack(window, list_b_src - (device - 1) * cells_b, list_b_off, offset_kinds)
    )
    every_b = jnp.ones((cells_b,), jnp.bool_)
    grouped_c = grouped_sum(mult_b, octant_b * cells_c + local_parent_b, every_b, cells_c)
    mult_c = apply_stack(m2m_ops, grouped_c).astype(jnp.bfloat16)
    shifted = per_cell(m2m_ops, mult_c, octant_c)
    top_table = (parent_c[:, None] == jnp.arange(top_cells, dtype=jnp.int32)[None, :]).astype(
        jnp.float32
    )
    partial_value = jnp.dot(
        shifted, top_table, precision=lax.Precision.HIGHEST, preferred_element_type=jnp.float32
    )
    top_mult = lax.psum(partial_value, ("leaf", "coef")).astype(jnp.bfloat16)
    top_local = apply_stack(m2l_ops, pack(top_mult, list_t_src, list_t_off, offset_kinds)).astype(
        jnp.bfloat16
    )
    parents_here = jnp.take(top_local, parent_c, axis=1)
    c_local = descend(m2m_ops, parents_here, jnp.arange(cells_c, dtype=jnp.int32), octant_c).astype(
        jnp.bfloat16
    )
    b_local = (near_b + descend(m2m_ops, c_local, local_parent_b, octant_b)).astype(jnp.bfloat16)
    fine_result = descend(m2m_ops, b_local, local_parent_a, octant_a)
    return jnp.where(living[None, :], fine_result, 0.0).astype(jnp.bfloat16)


def solution(mesh):
    in_specs = (
        P(None, ("leaf", "coef")),
        P(("leaf", "coef")),
        P(("leaf", "coef")),
        P(("leaf", "coef")),
        P(("leaf", "coef")),
        P(("leaf", "coef")),
        P(("leaf", "coef")),
        P(("leaf", "coef")),
        P(("leaf", "coef"), None),
        P(("leaf", "coef"), None),
        P(),
        P(),
        P(),
        P(),
    )
    out_specs = P(None, ("leaf", "coef"))
    return jax.shard_map(body, mesh=mesh, in_specs=in_specs, out_specs=out_specs, check_vma=False)
```

profile of v0, /device:TPU:1, one launch (start us, length us, event | category | flops | bytes accessed | tf_op | source)
XLA Modules:
  0.0 278.3 jit_solution(10299819700734533362)
XLA Ops:
  2.1 2.4 fusion.34
  5.5 3.1 %copy.59 = bf16[289,8,289]{0,1,2:T(8,128)(2,1)} copy(bf16[289,8,289]{2,1,0:T(8,128)(2,1)S(1)} %bitcast.114) | data formatting | bytes 2672672 | tf_op jit(solution)/shard_map/transpose | solution.py:31
  8.6 3.1 %fusion.51 = bf16[128,289]{0,1:T(8,128)(2,1)} fusion(bf16[289,8,289]{0,1,2:T(8,128)(2,1)} %copy.59, bf16[296,8,128]{2,1,0:T(8,128)(2,1)} %bitcast.120), kind=kOutput, calls=%fused_computation.37 | convolution fusion | flops 171088000 | bytes 2441472 | tf_op jit(solution)/shard_map/dot_general | solution.py:33
  11.7 3.9 %collective-permute-start = (bf16[289,128]{1,0:T(8,128)(2,1)}, bf16[289,128]{1,0:T(8,128)(2,1)}, u32[]{:S(2)}, u32[]{:S(2)}) collective-permute-start(bf16[289,128]{1,0:T(8,128)(2,1)} %bitcast.5), channel_id=1, source_target_pairs={{0,1},{1,2},{2,3},{3,4},{4,5},{5,6},{6,7},{7,8},{8,9},{9,10},{10,1... | collective-permute-start | bytes 221960 | tf_op jit(solution)/shard_map/ppermute | solution.py:14
  15.6 3.8 %collective-permute-start.1 = (bf16[289,128]{1,0:T(8,128)(2,1)}, bf16[289,128]{1,0:T(8,128)(2,1)}, u32[]{:S(2)}, u32[]{:S(2)}) collective-permute-start(bf16[289,128]{1,0:T(8,128)(2,1)} %bitcast.5), channel_id=1, source_target_pairs={{1,0},{2,1},{3,2},{4,3},{5,4},{6,5},{7,6},{8,7},{9,8},{10,9},{11,1... | collective-permute-start | bytes 221960 | tf_op jit(solution)/shard_map/ppermute | solution.py:15
  20.9 1.8 copy.75
  27.8 1.8 convolution_convert_fusion
  31.4 1.6 copy.65
  33.0 1.6 fusion.68
  38.1 110.6 %all-reduce.1 = bf16[289,1024]{1,0:T(8,128)(2,1)} all-reduce(f32[289,1024]{1,0:T(8,128)S(1)} %fusion.81), channel_id=1, replica_groups=mesh['leaf'=128,'coef'=4] {'leaf','coef'}, use_global_device_ids=true, to_apply=%region_0.1 | all-reduce | flops 295936 | bytes 1775616 | tf_op jit(solution)/shard_map/psum | solution.py:106
  150.6 2.5 copy.77
  153.3 65.3 %gather_fusion.1 = bf16[16384,289]{1,0:T(8,128)(2,1)} fusion(bf16[289,1024]{0,1:T(8,128)(2,1)S(1)} %copy.76, s32[16384]{0:T(1024)S(1)} %broadcast_clamp_fusion), kind=kCustom, calls=%fused_computation.1 | custom fusion | bytes 19005440 | tf_op jit(solution)/shard_map/jit(_take)/gather | solution.py:55
  218.7 7.3 %convert_bitcast_fusion = bf16[8,289,1024]{1,0,2:T(8,128)(2,1)S(1)} fusion(pred[1024,16,8]{1,2,0:T(8,128)(4,1)} %copy.77, bf16[289,1024,16]{0,2,1:T(8,128)(2,1)} %bitcast.118, pred[1024,16]{1,0:T(8,128)(4,1)S(1)} %copy.64), kind=kOutput, calls=%fused_computation.11 | convolution fusion | flops 82862080 | bytes 14352384 | tf_op jit(solution)/shard_map/ktj,tjo->okt/dot_general | solution.py:61
  226.0 3.3 %fusion.40 = bf16[289,1024]{1,0:T(8,128)(2,1)} fusion(bf16[289,8,289]{2,1,0:T(8,128)(2,1)S(1)} %bitcast.113, bf16[8,289,1024]{1,0,2:T(8,128)(2,1)S(1)} %convert_bitcast_fusion), kind=kOutput, calls=%fused_computation.33 | convolution fusion | flops 1368704000 | bytes 6663184 | tf_op jit(solution)/shard_map/dot_general | solution.py:33
  229.3 2.4 copy.80
  239.7 2.5 gather_fusion.2
  242.3 1.9 fusion.87
  244.2 2.2 gather_fusion.3
  246.4 1.9 fusion.85
  249.0 1.8 gather_fusion.4
  255.5 9.1 %gather_fusion = bf16[2048,289]{1,0:T(8,128)(2,1)} fusion(bf16[289,384]{0,1:T(8,128)(2,1)S(1)} %copy.61, s32[2048]{0:T(1024)S(1)} %copy-done.8), kind=kCustom, calls=%fused_computation | custom fusion | bytes 2375680 | tf_op jit(solution)/shard_map/jit(_take)/gather | solution.py:55
  264.6 3.0 %fusion.37 = bf16[8,289,128]{1,0,2:T(8,128)(2,1)} fusion(bf16[289,128,16]{0,2,1:T(8,128)(2,1)} %bitcast.121, pred[128,16]{1,0:T(8,128)(4,1)} %copy.58, s32[128,16]{1,0:T(8,128)} %copy.57), kind=kOutput, calls=%fused_computation.32 | convolution fusion | flops 10374144 | bytes 1785856 | tf_op jit(solution)/shard_map/ktj,tjo->okt/dot_general | solution.py:61
  267.6 3.4 %convolution_bitcast_fusion = bf16[289,8,128]{2,0,1:T(8,128)(2,1)} fusion(bf16[289,8,289]{2,1,0:T(8,128)(2,1)S(1)} %bitcast.112, bf16[8,289,128]{1,0,2:T(8,128)(2,1)} %fusion.37, f32[128,289]{0,1:T(8,128)} %copy.83, pred[128]{0:T(512)(128)(4,1)} %get-tuple-element.7, bf16[8,289,289]{2,0,1:T(8,128)(2,1)S(1)} %copy-done.3), kind=kOutput, calls=%fused_computation.28 | convolution fusion | flops 342212992 | bytes 4004512 | tf_op jit(solution)/shard_map/dot_general | solution.py:46
  272.5 4.4 %gather_fusion.5 = bf16[1024,289]{1,0:T(8,128)(2,1)S(1)} fusion(bf16[289,1024]{0,1:T(8,128)(2,1)S(1)} %bitcast.116, s32[1024]{0:T(1024)} %fusion.94), kind=kCustom, calls=%fused_computation.5 | custom fusion | bytes 1187840 | tf_op jit(solution)/shard_map/jit(_take)/gather | solution.py:50
  (71 shorter events, 32.4 us)
Async XLA Ops:
  0.0 226.0 %copy-start = (bf16[8,289,289]{2,0,1:T(8,128)(2,1)S(1)}, bf16[8,289,289]{2,0,1:T(8,128)(2,1)}, u32[]{:S(2)}) copy-start(bf16[8,289,289]{2,0,1:T(8,128)(2,1)} %param.27) | copy-start | bytes 4009012
  2.1 2.4 copy-start.9
  2.1 2.4 copy-start.11
  2.1 3.4 %copy-start.1 = (bf16[8,289,289]{2,0,1:T(8,128)(2,1)S(1)}, bf16[8,289,289]{2,0,1:T(8,128)(2,1)}, u32[]{:S(2)}) copy-start(bf16[8,289,289]{2,0,1:T(8,128)(2,1)} %param.26) | copy-start | bytes 4009012
  11.7 242.7 %collective-permute-start = (bf16[289,128]{1,0:T(8,128)(2,1)}, bf16[289,128]{1,0:T(8,128)(2,1)}, u32[]{:S(2)}, u32[]{:S(2)}) collective-permute-start(bf16[289,128]{1,0:T(8,128)(2,1)} %bitcast.5), channel_id=1, source_target_pairs={{0,1},{1,2},{2,3},{3,4},{4,5},{5,6},{6,7},{7,8},{8,9},{9,10},{10,1... | collective-permute-start | bytes 221960 | tf_op jit(solution)/shard_map/ppermute | solution.py:14
  15.6 238.7 %collective-permute-start.1 = (bf16[289,128]{1,0:T(8,128)(2,1)}, bf16[289,128]{1,0:T(8,128)(2,1)}, u32[]{:S(2)}, u32[]{:S(2)}) collective-permute-start(bf16[289,128]{1,0:T(8,128)(2,1)} %bitcast.5), channel_id=1, source_target_pairs={{1,0},{2,1},{3,2},{4,3},{5,4},{6,5},{7,6},{8,7},{9,8},{10,9},{11,1... | collective-permute-start | bytes 221960 | tf_op jit(solution)/shard_map/ppermute | solution.py:15
  33.0 2.9 %copy-start.4 = (bf16[8,289,289]{2,1,0:T(8,128)(2,1)S(1)}, bf16[8,289,289]{2,1,0:T(8,128)(2,1)}, u32[]{:S(2)}) copy-start(bf16[8,289,289]{2,1,0:T(8,128)(2,1)} %copy.67) | copy-start | bytes 4009012
  33.0 4.4 %copy-start.13 = (s32[16]{0:T(128)S(1)}, s32[16]{0:T(128)}, u32[]{:S(2)}) copy-start(s32[16]{0:T(128)} %param.20) | copy-start | bytes 196
  38.1 112.1 %copy-start.5 = (s32[1024,16]{1,0:T(8,128)S(1)}, s32[1024,16]{1,0:T(8,128)}, u32[]{:S(2)}) copy-start(s32[1024,16]{1,0:T(8,128)} %copy.75) | copy-start | bytes 196612
  148.7 1.8 copy-start.6
  148.7 4.4 %copy-start.7 = (pred[1024,16]{0,1:T(8,128)(4,1)S(1)}, pred[1024,16]{0,1:T(8,128)(4,1)}, u32[]{:S(2)}) copy-start(pred[1024,16]{0,1:T(8,128)(4,1)} %compare_and_fusion) | copy-start | bytes 49156
  229.3 13.0 %copy-start.2 = (bf16[8,289,289]{2,0,1:T(8,128)(2,1)S(1)}, bf16[8,289,289]{2,0,1:T(8,128)(2,1)}, u32[]{:S(2)}) copy-start(bf16[8,289,289]{2,0,1:T(8,128)(2,1)} %param.26) | copy-start | bytes 4009012
  248.4 7.2 %copy-start.8 = (s32[2048]{0:T(1024)S(1)}, s32[2048]{0:T(1024)}, u32[]{:S(2)}) copy-start(s32[2048]{0:T(1024)} %broadcast_clamp_fusion.1) | copy-start | bytes 24580
  264.6 3.0 %copy-start.3 = (bf16[8,289,289]{2,0,1:T(8,128)(2,1)S(1)}, bf16[8,289,289]{2,0,1:T(8,128)(2,1)}, u32[]{:S(2)}) copy-start(bf16[8,289,289]{2,0,1:T(8,128)(2,1)} %param.26) | copy-start | bytes 4009012
  272.4 4.4 %copy-start.10 = (pred[1024]{0:T(1024)(128)(4,1)S(1)}, pred[1024]{0:T(1024)(128)(4,1)}, u32[]{:S(2)}) copy-start(pred[1024]{0:T(1024)(128)(4,1)} %get-tuple-element.5) | copy-start | bytes 3076
  272.4 4.4 %copy-start.12 = (pred[1024]{0:T(1024)(128)(4,1)S(1)}, pred[1024]{0:T(1024)(128)(4,1)}, u32[]{:S(2)}) copy-start(pred[1024]{0:T(1024)(128)(4,1)} %copy-done.11) | copy-start | bytes 3076
where the time goes:
time: 280 us; the launch traced here: 278 us
  blocking collectives  111 us (40%)
  local copies, waits for them, and re-layouts  110 us (39%)
  matrix products  31.9 us (11%)
  other arithmetic  16.6 us (6%)
  starting transfers between devices  7.7 us (3%)
    psum x1, blocking collectives, body(): top_mult = lax.psum(partial_value, ('leaf', 'coef')).astype(jnp.bfloat16)  111 us
    gather x2, local copies, waits for them, and re-layouts, pack(): jnp.take(source, sources.reshape(-1), axis=1)  74.4 us
    dot_general x2, matrix products, pack(): jnp.einsum('ktj,tjo->okt', gathered, one_hot, preferred_element_type=jnp....  10.3 us
    gather x4, local copies, waits for them, and re-layouts, descend(): return jnp.take(products, octant * width + parent, axis=1)  9.15 us
    dot_general x3, matrix products, apply_stack(): return jnp.dot(joined_ops, joined_stack, preferred_element_type=jnp.float32)  7.99 us
    dot_general x3, matrix products, descend(): lax.dot_general(operators, source, (((1,), (0,)), ((), ())), preferred_el...  7.24 us
    unnamed x32, local copies, waits for them, and re-layouts  5.74 us
  transfers between devices with their start and end apart: 2, of which 0 were waited for; matrix products, arithmetic and copies ran while one was open for 45% of the time, Pallas kernels for 0%

commit v1 on v0

v1 whole, which is shorter than its diff:
```python
import functools

import jax
import jax.numpy as jnp
from jax import lax
from jax.experimental import pallas as pl
from jax.experimental.pallas import tpu as pltpu
from jax.sharding import PartitionSpec as P

MESH = pl.DeviceIdType.MESH
F32 = jnp.float32
BF16 = jnp.bfloat16
I32 = jnp.int32
LANES = 128
CORES = 2


def dot(a, b, contract=(1, 0)):
    return lax.dot_general(
        a, b, (((contract[0],), (contract[1],)), ((), ())), preferred_element_type=F32
    )


def column_of(row):
    n = row.shape[1]
    diagonal = lax.broadcasted_iota(I32, (n, n), 0) == lax.broadcasted_iota(I32, (n, n), 1)
    return jnp.sum(jnp.where(diagonal, row, 0), axis=1, keepdims=True)


def kernel(
    dims,
    leaf_hbm,
    count_ref,
    pa_ref,
    oa_ref,
    pb_ref,
    ob_ref,
    pc_ref,
    oc_ref,
    lbs_ref,
    lbo_ref,
    lts_ref,
    lto_ref,
    m2m_hbm,
    m2l_hbm,
    out_ref,
    leaf_v,
    m2m_v,
    m2l_v,
    one_hot_a,
    grouped_v,
    window,
    near_t,
    pad_v,
    count_b,
    count_t,
    packed_v,
    recv1,
    send2,
    recv2,
    recv3,
    recv4,
    send5,
    recv5,
    prod_c,
    prod_b,
    load_sem,
    near_send,
    near_recv,
    send_sem,
    recv_sem,
):
    ny, nz, nx = dims
    na = CORES * nx
    k = leaf_v.shape[0]
    cells_a = leaf_v.shape[1]
    cells_b = pb_ref.shape[1]
    cells_c = pc_ref.shape[1]
    entries, tops = lts_ref.shape
    kinds = m2l_v.shape[0]
    kp = recv1.shape[1]

    leaf_i, x = lax.axis_index("leaf"), lax.axis_index("coef")
    device = leaf_i * nx + x
    devices = ny * nz * na
    core = lax.rem(leaf_i, CORES)
    z = lax.rem(leaf_i // CORES, nz)
    y = leaf_i // (CORES * nz)
    a = core * nx + x

    def at(yy, zz, aa):
        return ((yy * nz + zz) * CORES + aa // nx, lax.rem(aa, nx))

    def linear(d):
        return (d // nx, lax.rem(d, nx))

    group_a = [lax.rem(a + i, na) for i in range(1, na)]
    group_z = [lax.rem(z + i, nz) for i in range(1, nz)]
    group_y = [lax.rem(y + i, ny) for i in range(1, ny)]
    before = linear(lax.rem(device + devices - 1, devices))
    after = linear(lax.rem(device + 1, devices))

    loads = [
        pltpu.make_async_copy(leaf_hbm, leaf_v, load_sem.at[0]),
        pltpu.make_async_copy(m2m_hbm, m2m_v, load_sem.at[1]),
        pltpu.make_async_copy(m2l_hbm, m2l_v, load_sem.at[2]),
    ]
    for load in loads:
        load.start()

    barrier = pltpu.get_barrier_semaphore()
    partners = (
        [at(y, z, aa) for aa in group_a]
        + [at(y, zz, a) for zz in group_z]
        + [at(yy, z, a) for yy in group_y]
        + [before, after]
    )
    for partner in partners:
        pl.semaphore_signal(barrier, inc=1, device_id=partner, device_id_type=MESH)

    cell = (
        lax.broadcasted_iota(I32, pa_ref.shape, 0) * LANES
        + lax.broadcasted_iota(I32, pa_ref.shape, 1)
    )
    code_a = oa_ref[...] * cells_b + pa_ref[...] - device * cells_b
    code_a = jnp.where(cell < count_ref[0], code_a, -1)
    slot = lax.broadcasted_iota(I32, (8 * cells_b, LANES), 0)
    for r in range(cells_a // LANES):
        one_hot_a[:, r * LANES : (r + 1) * LANES] = (slot == code_a[r : r + 1, :]).astype(F32).astype(BF16)

    loads[0].wait()
    for o in range(8):
        rows = slice(o * cells_b, (o + 1) * cells_b)
        grouped_v[:, rows] = dot(leaf_v[...], one_hot_a[rows, :], (1, 1)).astype(BF16)
    loads[1].wait()
    mult_b = dot(m2m_v[0], grouped_v[:, :cells_b])
    for o in range(1, 8):
        mult_b = mult_b + dot(m2m_v[o], grouped_v[:, o * cells_b : (o + 1) * cells_b])
    mult_b = mult_b.astype(BF16)
    window[:, cells_b : 2 * cells_b] = jnp.zeros((window.shape[0], cells_b), BF16)
    window[0:k, cells_b : 2 * cells_b] = mult_b

    pl.semaphore_wait(barrier, len(partners))

    mine = window.at[:, cells_b : 2 * cells_b]
    to_before = pltpu.make_async_remote_copy(
        src_ref=mine,
        dst_ref=window.at[:, 2 * cells_b : 3 * cells_b],
        send_sem=near_send.at[0],
        recv_sem=near_recv.at[0],
        device_id=before,
        device_id_type=MESH,
    )
    to_after = pltpu.make_async_remote_copy(
        src_ref=mine,
        dst_ref=window.at[:, 0:cells_b],
        send_sem=near_send.at[1],
        recv_sem=near_recv.at[1],
        device_id=after,
        device_id_type=MESH,
    )
    to_before.start()
    to_after.start()

    code_b = ob_ref[...] * cells_c + pb_ref[...] - device * cells_c
    slots_b = 8 * cells_c
    one_hot_b = (lax.broadcasted_iota(I32, (slots_b, cells_b), 0) == code_b).astype(F32)
    grouped_c = dot(mult_b, one_hot_b.astype(BF16), (1, 1)).astype(BF16)
    mult_c = dot(m2m_v[0], grouped_c[:, :cells_c])
    for o in range(1, 8):
        mult_c = mult_c + dot(m2m_v[o], grouped_c[:, o * cells_c : (o + 1) * cells_c])
    octant_c = oc_ref[...]
    shifted = jnp.zeros((k, cells_c), F32)
    for o in range(8):
        shifted = shifted + dot(m2m_v[o], jnp.where(octant_c == o, mult_c, 0.0).astype(BF16))
    pad_v[...] = jnp.zeros(pad_v.shape, F32)
    pad_v[0:k, 0:cells_c] = shifted
    shifted_t = pad_v[...].T[0:cells_c, :]
    parent_c = column_of(pc_ref[...])
    octant_c = column_of(octant_c)
    lane = lax.broadcasted_iota(I32, (cells_c, kp), 1)
    message = jnp.where(
        lane == k,
        (parent_c // 32).astype(F32),
        jnp.where(lane == k + 1, (parent_c % 32).astype(F32), shifted_t),
    )

    def block(ref, i, rows):
        return ref.at[pl.ds(pl.multiple_of(i * rows, rows), rows)]

    def stage(number, partner_ids, positions, source, target, place, rows):
        copies = []
        for i, (partner, position) in enumerate(zip(partner_ids, positions)):
            src = block(target, place, rows) if source is None else block(source, position, rows)
            copy = pltpu.make_async_remote_copy(
                src_ref=src,
                dst_ref=block(target, place, rows),
                send_sem=send_sem.at[number, i],
                recv_sem=recv_sem.at[number, i],
                device_id=partner,
                device_id_type=MESH,
            )
            copy.start()
            copies.append(copy)
        return copies

    def arrive(copies):
        for copy in copies:
            copy.wait_recv()

    def total(ref, parts, rows):
        summed = ref[0:rows, :].astype(F32)
        for i in range(1, parts):
            summed = summed + ref[i * rows : (i + 1) * rows, :].astype(F32)
        return summed

    ids_a = [at(y, z, aa) for aa in group_a]
    ids_z = [at(y, zz, a) for zz in group_z]
    ids_y = [at(yy, z, a) for yy in group_y]
    rows = cells_c
    own_tops = tops // (nz * na)

    block(recv1, a, rows)[...] = message.astype(BF16)
    copies1 = stage(0, ids_a, group_a, None, recv1, a, rows)

    base = (device - 1) * cells_b
    source_id = lbs_ref[...] - base
    kind = lbo_ref[...]
    place_b = lax.broadcasted_iota(I32, (3 * cells_b, cells_b), 0)
    for o in range(kinds):
        keyed = jnp.where(kind == o, source_id, -1)
        counts = jnp.zeros((3 * cells_b, cells_b), F32)
        for e in range(entries):
            counts = counts + (place_b == keyed[e : e + 1, :]).astype(F32)
        count_b[:, o * cells_b : (o + 1) * cells_b] = counts.astype(BF16)

    arrive(copies1)
    gathered = recv1[...]
    high = gathered[:, k : k + 1].astype(F32)
    low = gathered[:, k + 1 : k + 2].astype(F32)
    parent = high * 32.0 + low
    targets = na * cells_c
    sets = nz * own_tops
    spot = lax.broadcasted_iota(I32, (targets, sets), 1)
    spot = (spot // own_tops) * (na * own_tops) + a * own_tops + spot % own_tops
    member = (parent == spot.astype(F32)).astype(F32).astype(BF16)
    send2[...] = dot(member, gathered, (0, 0)).astype(BF16)

    block(recv2, z, own_tops)[...] = block(send2, z, own_tops)[...]
    copies2 = stage(1, ids_z, group_z, send2, recv2, z, own_tops)

    listed = lto_ref[...] * tops + lts_ref[...]
    parts = jnp.concatenate([(listed // 128).astype(F32), (listed % 128).astype(F32)], axis=0)
    parent_hot = (parent == lax.broadcasted_iota(I32, (targets, tops), 1).astype(F32)).astype(F32)
    codes = dot(parts.astype(BF16), parent_hot.astype(BF16), (1, 1))
    codes = codes[0:entries, :] * 128.0 + codes[entries:, :]
    spot_t = lax.broadcasted_iota(I32, (sets, targets), 0)
    spot_t = (spot_t // own_tops) * (na * own_tops) + a * own_tops + spot_t % own_tops
    for o in range(kinds):
        wanted = (spot_t + o * tops).astype(F32)
        counts = jnp.zeros((sets, targets), F32)
        for e in range(entries):
            counts = counts + (wanted == codes[e : e + 1, :]).astype(F32)
        count_t[:, o * targets : (o + 1) * targets] = counts.astype(BF16)

    arrive(copies2)
    block(recv3, y, own_tops)[...] = total(recv2, nz, own_tops).astype(BF16)

    copies3 = stage(2, ids_y, group_y, None, recv3, y, own_tops)
    arrive(copies3)
    block(recv4, z, own_tops)[...] = total(recv3, ny, own_tops).astype(BF16)

    copies4 = stage(3, ids_z, group_z, None, recv4, z, own_tops)

    loads[2].wait()
    to_before.wait_recv()
    to_after.wait_recv()
    near = jnp.zeros((k, cells_b), F32)
    for o in range(kinds):
        packed = dot(window[0:k, :], count_b[:, o * cells_b : (o + 1) * cells_b]).astype(BF16)
        near = near + dot(m2l_v[o], packed)
    pad_v[0:k, :] = near
    near_t[...] = pad_v[...].T

    arrive(copies4)
    packed_v[...] = dot(recv4[...], count_t[...], (0, 0)).astype(BF16)
    partial = dot(m2l_v[0], packed_v[0:k, 0:targets])
    for o in range(1, kinds):
        partial = partial + dot(m2l_v[o], packed_v[0:k, o * targets : (o + 1) * targets])
    pad_v[0:k, 0:targets] = partial
    send5[...] = pad_v[...].T[0:targets, :].astype(BF16)

    block(recv5, a, rows)[...] = block(send5, a, rows)[...]
    copies5 = stage(4, ids_a, group_a, send5, recv5, a, rows)
    one_hot_bt = one_hot_b.T.astype(BF16)
    arrive(copies5)
    top_local = total(recv5, na, rows).astype(BF16)[:, 0:k]

    local_c = jnp.zeros((cells_c, k), F32)
    for o in range(8):
        local_c = local_c + jnp.where(octant_c == o, dot(top_local, m2m_v[o]), 0.0)
    local_c = local_c.astype(BF16)
    for o in range(8):
        prod_c[o * cells_c : (o + 1) * cells_c, :] = dot(local_c, m2m_v[o])
    full = prod_c[...]
    rounded = full.astype(BF16)
    rest = (full - rounded.astype(F32)).astype(BF16)
    far = dot(one_hot_bt, rounded) + dot(one_hot_bt, rest)
    local_b = (near_t[:, 0:k] + far).astype(BF16)
    for o in range(8):
        prod_b[o * cells_b : (o + 1) * cells_b, :] = dot(local_b, m2m_v[o]).astype(BF16)
    out_ref[...] = dot(prod_b[...], one_hot_a[...], (0, 0)).astype(BF16)

    to_before.wait_send()
    to_after.wait_send()
    for copy in copies1 + copies2 + copies3 + copies4 + copies5:
        copy.wait_send()


def body(dims, *args):
    (
        leaf_mult,
        fine_count,
        parent_a,
        octant_a,
        parent_b,
        octant_b,
        parent_c,
        octant_c,
        list_b_src,
        list_b_off,
        list_t_src,
        list_t_off,
        m2m_ops,
        m2l_ops,
    ) = args
    ny, nz, nx = dims
    na = CORES * nx
    k, cells_a = leaf_mult.shape
    cells_b = parent_b.shape[0]
    cells_c = parent_c.shape[0]
    tops = list_t_src.shape[0]
    kinds = m2l_ops.shape[0]
    kp = -(-(k + 2) // LANES) * LANES
    kr = -(-k // 16) * 16
    own_tops = tops // (nz * na)
    targets = na * cells_c
    sets = nz * own_tops
    wide = max(cells_b, targets)
    vmem = pl.BlockSpec(memory_space=pltpu.VMEM)
    smem = pl.BlockSpec(memory_space=pltpu.SMEM)
    hbm = pl.BlockSpec(memory_space=pl.ANY)
    most = max(na, nz, ny) - 1
    fine = pl.pallas_call(
        functools.partial(kernel, dims),
        out_shape=jax.ShapeDtypeStruct((k, cells_a), BF16),
        in_specs=[hbm, smem] + [vmem] * 10 + [hbm, hbm],
        out_specs=vmem,
        scratch_shapes=[
            pltpu.VMEM((k, cells_a), BF16),
            pltpu.VMEM(m2m_ops.shape, BF16),
            pltpu.VMEM(m2l_ops.shape, BF16),
            pltpu.VMEM((8 * cells_b, cells_a), BF16),
            pltpu.VMEM((k, 8 * cells_b), BF16),
            pltpu.VMEM((kr, 3 * cells_b), BF16),
            pltpu.VMEM((cells_b, kp), F32),
            pltpu.VMEM((kp, wide), F32),
            pltpu.VMEM((3 * cells_b, kinds * cells_b), BF16),
            pltpu.VMEM((sets, kinds * targets), BF16),
            pltpu.VMEM((kp, kinds * targets), BF16),
            pltpu.VMEM((targets, kp), BF16),
            pltpu.VMEM((sets, kp), BF16),
            pltpu.VMEM((sets, kp), BF16),
            pltpu.VMEM((ny * own_tops, kp), BF16),
            pltpu.VMEM((sets, kp), BF16),
            pltpu.VMEM((targets, kp), BF16),
            pltpu.VMEM((targets, kp), BF16),
            pltpu.VMEM((8 * cells_c, k), F32),
            pltpu.VMEM((8 * cells_b, k), BF16),
            pltpu.SemaphoreType.DMA((3,)),
            pltpu.SemaphoreType.DMA((2,)),
            pltpu.SemaphoreType.DMA((2,)),
            pltpu.SemaphoreType.DMA((5, most)),
            pltpu.SemaphoreType.DMA((5, most)),
        ],
        compiler_params=pltpu.CompilerParams(
            collective_id=0, has_side_effects=True, vmem_limit_bytes=48 * 1024 * 1024
        ),
    )(
        leaf_mult,
        fine_count,
        parent_a.reshape(-1, LANES),
        octant_a.reshape(-1, LANES),
        parent_b.reshape(1, -1),
        octant_b.reshape(1, -1),
        parent_c.reshape(1, -1),
        octant_c.reshape(1, -1),
        list_b_src.T,
        list_b_off.T,
        list_t_src.T,
        list_t_off.T,
        m2m_ops,
        m2l_ops,
    )
    return fine


def solution(mesh):
    nx = mesh.shape["coef"]
    plane = mesh.shape["leaf"] // CORES
    nz = 1
    while nz * nz < plane:
        nz *= 2
    both = P(("leaf", "coef"))
    rows = P(("leaf", "coef"), None)
    in_specs = (P(None, ("leaf", "coef")),) + (both,) * 7 + (rows, rows) + (P(),) * 4
    return jax.shard_map(
        functools.partial(body, (plane // nz, nz, nx)),
        mesh=mesh,
        in_specs=in_specs,
        out_specs=P(None, ("leaf", "coef")),
        check_vma=False,
    )
```

time: 280 us -> 55 us (0.20)
  blocking collectives: 111 us -> 0 us
  local copies, waits for them, and re-layouts: 110 us -> 3.54 us
  Pallas kernels: 0 us -> 50.4 us
  matrix products: 31.9 us -> 0 us
  other arithmetic: 16.6 us -> 0 us
  starting transfers between devices: 7.7 us -> 0 us
    psum x1 -> x0, blocking collectives: 111 us -> none  [body(): top_mult = lax.psum(partial_value, ('leaf', 'coef')).astype(jnp.bfloat16)]
    gather x7 -> x0, local copies, waits for them, and re-layouts: 86.1 us -> none  [the longest x2 74.4 us: pack(): jnp.take(source, sources.reshape(-1), axis=1)]
    pallas_call x0 -> x1, Pallas kernels: none -> 50.4 us  [body(): pl.pallas_call(functools.partial(kernel, dims), out_shape=jax.ShapeDtypeS...]
    dot_general x19 -> x0, matrix products: 31.9 us -> none  [the longest x2 10.3 us: pack(): jnp.einsum('ktj,tjo->okt', gathered, one_hot, preferred_element_type=jnp....]
    and x6 -> x0, other arithmetic: 7.74 us -> none  [the longest x3 3.76 us: descend(): return jnp.take(products, octant * width + parent, axis=1)]
    ppermute x2 -> x0, starting transfers between devices: 7.7 us -> none  [the longest x1 3.95 us: padded(): before = lax.ppermute(last, axis, up)]
    convert_element_type x4 -> x0, local copies, waits for them, and re-layouts: 6.55 us -> none  [the longest x1 2.37 us: body(): apply_stack(m2l_ops, pack(top_mult, list_t_src, list_t_off, offset_kinds))]
    gather x6 -> x0, other arithmetic: 4.99 us -> none  [the longest x3 3.15 us: descend(): return jnp.take(products, octant * width + parent, axis=1)]
  transfers between devices with their start and end apart: 2 -> 0, of which waited for: 0 -> 0; matrix products, arithmetic and copies ran while one was open for 45% -> 0% of each run, Pallas kernels for 0% -> 0%
where the time goes in v1:
time: 55 us; the launch traced here: 54.8 us
  Pallas kernels  50.4 us (92%)
  local copies, waits for them, and re-layouts  3.54 us (6%)
  between operations  0.95 us (2%)
    pallas_call x1, Pallas kernels, body(): pl.pallas_call(functools.partial(kernel, dims), out_shape=jax.ShapeDtypeS...  50.4 us
    unnamed x27, local copies, waits for them, and re-layouts  3.54 us

profile of v1, /device:TPU:1, one launch (start us, length us, event | category | flops | bytes accessed | tf_op | source)
XLA Modules:
  0.0 54.8 jit_solution(17575625504667233199)
XLA Ops:
  0.8 1.7 %copy.15.m2m_hbm = bf16[8,289,289]{2,1,0:T(8,128)(2,1)S(1)} copy(bf16[8,289,289]{2,0,1:T(8,128)(2,1)} %param.26) | data formatting | bytes 2672672 | tf_op args[12]
  2.5 0.0 copy-done.11
  2.5 0.0 copy-start
  2.5 0.0 copy-start.1
  2.5 0.0 copy-start.2
  2.5 0.0 copy-start.3
  2.6 0.0 copy-start.4
  2.6 0.0 copy-start.5
  2.6 0.0 copy-start.6
  2.6 0.0 copy-start.7
  2.6 0.0 copy-start.8
  2.6 0.0 copy-start.9
  2.6 0.0 copy-start.10
  2.6 0.2 copy.16.m2l_hbm
  2.9 0.7 %copy-done = bf16[289,1024]{1,0:T(8,128)(2,1)S(1)} copy-done((bf16[289,1024]{1,0:T(8,128)(2,1)S(1)}, bf16[289,1024]{1,0:T(8,128)(2,1)}, u32[]{:S(2)}) %copy-start) | copy-done | bytes 591896
  3.6 0.0 copy-done.1
  3.6 0.0 copy-done.2
  3.6 0.0 copy-done.3
  3.6 0.0 copy-done.4
  3.6 0.0 copy-done.5
  3.6 0.0 copy-done.6
  3.6 0.0 copy-done.7
  3.7 50.4 %shard_map.136 = bf16[289,1024]{1,0:T(8,128)(2,1)S(1)} custom-call(bf16[289,1024]{1,0:T(8,128)(2,1)S(1)} %copy-done, s32[1]{0:T(128)S(6)} %copy.18.count_ref, s32[8,128]{1,0:T(8,128)S(1)} %bitcast.14, s32[8,128]{1,0:T(8,128)S(1)} %bitcast.15, s32[1,128]{1,0:T(1,128)S(1)} %bitcast.16, s32[1,128]{1,0:T(1,128)S(1)} %bitcast.17, s32[1,16]{1,0:T(1,128)S(1)} %bitcast.18, ...), custom_call_target="tpu_custom_call" | custom-call | tf_op jit(solution)/shard_map/pallas_call | solution.py:354
  54.0 0.8 %copy.19 = bf16[289,1024]{1,0:T(8,128)(2,1)} copy(bf16[289,1024]{1,0:T(8,128)(2,1)S(1)} %shard_map.136) | data formatting | bytes 1183744
  (4 shorter events, 0.0 us)
Async XLA Ops:
  0.0 2.5 %copy-start.11 = (bf16[8,289,289]{2,0,1:T(8,128)(2,1)S(1)}, bf16[8,289,289]{2,0,1:T(8,128)(2,1)}, u32[]{:S(2)}) copy-start(bf16[8,289,289]{2,0,1:T(8,128)(2,1)} %param.27) | copy-start | bytes 4009012
  2.5 1.1 %copy-start = (bf16[289,1024]{1,0:T(8,128)(2,1)S(1)}, bf16[289,1024]{1,0:T(8,128)(2,1)}, u32[]{:S(2)}) copy-start(bf16[289,1024]{1,0:T(8,128)(2,1)} %leaf_hbm.1) | copy-start | bytes 1775620
  2.5 1.1 %copy-start.1 = (s32[1024,16]{0,1:T(8,128)S(1)}, s32[1024,16]{0,1:T(8,128)}, u32[]{:S(2)}) copy-start(s32[1024,16]{0,1:T(8,128)} %param.24) | copy-start | bytes 196612
  2.5 1.1 %copy-start.2 = (s32[1024,16]{0,1:T(8,128)S(1)}, s32[1024,16]{0,1:T(8,128)}, u32[]{:S(2)}) copy-start(s32[1024,16]{0,1:T(8,128)} %param.25) | copy-start | bytes 196612
  2.5 1.0 %copy-start.3 = (s32[128,16]{0,1:T(8,128)S(1)}, s32[128,16]{0,1:T(8,128)}, u32[]{:S(2)}) copy-start(s32[128,16]{0,1:T(8,128)} %param.22) | copy-start | bytes 24580
  2.6 1.0 %copy-start.4 = (s32[128,16]{0,1:T(8,128)S(1)}, s32[128,16]{0,1:T(8,128)}, u32[]{:S(2)}) copy-start(s32[128,16]{0,1:T(8,128)} %param.23) | copy-start | bytes 24580
  2.6 1.0 %copy-start.5 = (s32[1024]{0:T(1024)S(1)}, s32[1024]{0:T(1024)}, u32[]{:S(2)}) copy-start(s32[1024]{0:T(1024)} %param.16) | copy-start | bytes 12292
  2.6 1.0 %copy-start.6 = (s32[1024]{0:T(1024)S(1)}, s32[1024]{0:T(1024)}, u32[]{:S(2)}) copy-start(s32[1024]{0:T(1024)} %param.17) | copy-start | bytes 12292
  2.6 1.0 %copy-start.7 = (s32[128]{0:T(128)S(1)}, s32[128]{0:T(128)}, u32[]{:S(2)}) copy-start(s32[128]{0:T(128)} %param.18) | copy-start | bytes 1540
  2.6 1.0 %copy-start.8 = (s32[128]{0:T(128)S(1)}, s32[128]{0:T(128)}, u32[]{:S(2)}) copy-start(s32[128]{0:T(128)} %param.19) | copy-start | bytes 1540
  2.6 1.0 %copy-start.9 = (s32[16]{0:T(128)S(1)}, s32[16]{0:T(128)}, u32[]{:S(2)}) copy-start(s32[16]{0:T(128)} %param.20) | copy-start | bytes 196
  2.6 1.0 %copy-start.10 = (s32[16]{0:T(128)S(1)}, s32[16]{0:T(128)}, u32[]{:S(2)}) copy-start(s32[16]{0:T(128)} %param.21) | copy-start | bytes 196

commit v2 on v1

v2 whole, which is shorter than its diff:
```python
import functools

import jax
import jax.numpy as jnp
from jax import lax
from jax.experimental import pallas as pl
from jax.experimental.pallas import tpu as pltpu
from jax.sharding import PartitionSpec as P

MESH = pl.DeviceIdType.MESH
F32 = jnp.float32
BF16 = jnp.bfloat16
I32 = jnp.int32
LANES = 128
CORES = 2


def dot(a, b, contract=(1, 0)):
    return lax.dot_general(
        a, b, (((contract[0],), (contract[1],)), ((), ())), preferred_element_type=F32
    )


def column_of(row):
    n = row.shape[1]
    diagonal = lax.broadcasted_iota(I32, (n, n), 0) == lax.broadcasted_iota(I32, (n, n), 1)
    return jnp.sum(jnp.where(diagonal, row, 0), axis=1, keepdims=True)


def kernel(
    dims,
    leaf_hbm,
    count_ref,
    pa_ref,
    oa_ref,
    pb_ref,
    ob_ref,
    pc_ref,
    oc_ref,
    lbs_ref,
    lbo_ref,
    lts_ref,
    lto_ref,
    m2m_hbm,
    m2l_hbm,
    out_ref,
    leaf_v,
    m2m_v,
    m2l_v,
    one_hot_a,
    grouped_v,
    window,
    near_t,
    pad_v,
    count_b,
    count_t,
    gathered,
    turned,
    heads,
    shares,
    arrived,
    prod_c,
    prod_b,
    load_sem,
    near_send,
    near_recv,
    sems_z,
    sems_x,
    sems_h,
    sems_q,
):
    ny, nz, nx = dims
    k = leaf_v.shape[0]
    cells_a = leaf_v.shape[1]
    cells_b = pb_ref.shape[1]
    cells_c = pc_ref.shape[1]
    entries, tops = lts_ref.shape
    kinds = m2l_v.shape[0]
    kp = gathered.shape[1]

    leaf_i, x = lax.axis_index("leaf"), lax.axis_index("coef")
    device = leaf_i * nx + x
    devices = ny * nz * CORES * nx
    core = lax.rem(leaf_i, CORES)
    z = lax.rem(leaf_i // CORES, nz)
    y = leaf_i // (CORES * nz)

    def at(dy, dz, dc, dx):
        yy, zz = lax.rem(y + dy + ny, ny), lax.rem(z + dz + nz, nz)
        cc, xx = lax.rem(core + dc + CORES, CORES), lax.rem(x + dx + nx, nx)
        return ((yy * nz + zz) * CORES + cc, xx)

    def linear(d):
        return (d // nx, lax.rem(d, nx))

    steps_z = sorted(range(nz), key=lambda i: (min(i, nz - i), i))
    steps_x = range(nx)
    steps_q = sorted(
        [(i, c) for i in range(ny) for c in range(CORES)], key=lambda s: (min(s[0], ny - s[0]), s)
    )
    before = linear(lax.rem(device + devices - 1, devices))
    after = linear(lax.rem(device + 1, devices))

    loads = [
        pltpu.make_async_copy(leaf_hbm, leaf_v, load_sem.at[0]),
        pltpu.make_async_copy(m2m_hbm, m2m_v, load_sem.at[1]),
        pltpu.make_async_copy(m2l_hbm, m2l_v, load_sem.at[2]),
    ]
    for load in loads:
        load.start()

    barrier = pltpu.get_barrier_semaphore()
    partners = (
        [at(0, j, 0, 0) for j in steps_z if j]
        + [at(0, 0, 0, i) for i in steps_x if i]
        + [at(j, 0, c, 0) for j, c in steps_q if j or c]
        + [before, after]
    )
    for partner in partners:
        pl.semaphore_signal(barrier, inc=1, device_id=partner, device_id_type=MESH)

    cell = (
        lax.broadcasted_iota(I32, pa_ref.shape, 0) * LANES
        + lax.broadcasted_iota(I32, pa_ref.shape, 1)
    )
    code_a = oa_ref[...] * cells_b + pa_ref[...] - device * cells_b
    code_a = jnp.where(cell < count_ref[0], code_a, -1)
    slot = lax.broadcasted_iota(I32, (8 * cells_b, LANES), 0)
    for r in range(cells_a // LANES):
        one_hot_a[:, r * LANES : (r + 1) * LANES] = (slot == code_a[r : r + 1, :]).astype(F32).astype(BF16)

    loads[0].wait()
    for o in range(0, 8, 2):
        rows = slice(o * cells_b, (o + 2) * cells_b)
        grouped_v[:, rows] = dot(leaf_v[...], one_hot_a[rows, :], (1, 1)).astype(BF16)
    loads[1].wait()
    mult_b = dot(m2m_v[0], grouped_v[:, :cells_b])
    for o in range(1, 8):
        mult_b = mult_b + dot(m2m_v[o], grouped_v[:, o * cells_b : (o + 1) * cells_b])
    mult_b = mult_b.astype(BF16)
    window[:, cells_b : 2 * cells_b] = jnp.zeros((window.shape[0], cells_b), BF16)
    window[0:k, cells_b : 2 * cells_b] = mult_b

    code_b = ob_ref[...] * cells_c + pb_ref[...] - device * cells_c
    slots_b = 8 * cells_c
    one_hot_b = (lax.broadcasted_iota(I32, (slots_b, cells_b), 0) == code_b).astype(F32)
    grouped_c = dot(mult_b, one_hot_b.astype(BF16), (1, 1)).astype(BF16)
    mult_c = dot(m2m_v[0], grouped_c[:, :cells_c])
    for o in range(1, 8):
        mult_c = mult_c + dot(m2m_v[o], grouped_c[:, o * cells_c : (o + 1) * cells_c])
    octant_c = oc_ref[...]
    shifted = jnp.zeros((k, cells_c), F32)
    for o in range(8):
        shifted = shifted + dot(m2m_v[o], jnp.where(octant_c == o, mult_c, 0.0).astype(BF16))
    pad_v[...] = jnp.zeros(pad_v.shape, F32)
    pad_v[0:k, 0:cells_c] = shifted
    shifted_t = pad_v[:, 0:LANES].T[0:cells_c, :]
    parent_c = column_of(pc_ref[...])
    octant_c = column_of(octant_c)
    high = (parent_c // 32).astype(F32)
    low = (parent_c % 32).astype(F32)
    lane = lax.broadcasted_iota(I32, (cells_c, kp), 1)
    message = jnp.where(lane == k, high, jnp.where(lane == k + 1, low, shifted_t))
    gathered[0:cells_c, :] = message.astype(BF16)
    lane = lax.broadcasted_iota(I32, (cells_c, LANES), 1)
    heads[0:cells_c, :] = jnp.where(lane < LANES // 2, high, low).astype(BF16)

    def send(src, dst, sems, index, partner):
        copy = pltpu.make_async_remote_copy(
            src_ref=src,
            dst_ref=dst,
            send_sem=sems[0].at[index],
            recv_sem=sems[1].at[index],
            device_id=partner,
            device_id_type=MESH,
        )
        copy.start()
        return copy

    def part(ref, i):
        return ref.at[i * cells_c : (i + 1) * cells_c]

    pl.semaphore_wait(barrier, len(partners))

    sent_z = {}
    for n, j in enumerate(steps_z):
        if j:
            sent_z[n] = send(part(gathered, 0), part(gathered, n * nx), sems_z, n - 1, at(0, j, 0, 0))
    sent_x = {}

    def spread(n):
        for i in steps_x:
            if i:
                sent_x[n, i] = send(
                    part(gathered, n * nx), part(gathered, n * nx + i), sems_x, n * (nx - 1) + i - 1, at(0, 0, 0, i)
                )

    spread(0)
    sent_heads = {}
    for n, (j, c) in enumerate(steps_q):
        if n:
            sent_heads[n] = send(part(heads, 0), part(heads, n), sems_h, n - 1, at(j, 0, c, 0))
    mine = window.at[:, cells_b : 2 * cells_b]
    near_sems = (near_send, near_recv)
    to_before = send(mine, window.at[:, 2 * cells_b : 3 * cells_b], near_sems, 0, before)
    to_after = send(mine, window.at[:, 0:cells_b], near_sems, 1, after)

    def count(place, wanted, kind, store):
        weights = []
        for first in range(0, kinds, 4):
            weight = jnp.zeros(kind.shape, I32)
            for o in range(first, min(first + 4, kinds)):
                weight = jnp.where(kind == o, 1 << (8 * (o - first)), weight)
            weights.append(weight)
        sums = [jnp.zeros((place.shape[0], kind.shape[1]), I32) for _ in weights]
        for e in range(entries):
            same = place == wanted[e : e + 1, :]
            sums = [s + jnp.where(same, w[e : e + 1, :], 0) for s, w in zip(sums, weights)]
        for o in range(kinds):
            store(o, ((sums[o // 4] >> (8 * (o % 4))) & 255).astype(F32).astype(BF16))

    def store_b(o, m):
        count_b[:, o * cells_b : (o + 1) * cells_b] = m

    place_b = lax.broadcasted_iota(I32, (3 * cells_b, cells_b), 0)
    count(place_b, lbs_ref[...] - (device - 1) * cells_b, lbo_ref[...], store_b)

    for n in range(1, nz):
        sent_z[n].wait_recv()
        spread(n)

    for n in sent_heads:
        sent_heads[n].wait_recv()
    targets = heads.shape[0]

    def parents(high, low):
        return (high.astype(F32) * 32.0 + low.astype(F32)).astype(I32)

    listed = lto_ref[...] * tops + lts_ref[...]
    split = jnp.concatenate([(listed // 128).astype(F32), (listed % 128).astype(F32)], axis=0)
    wanted = parents(heads[:, 0:1], heads[:, LANES // 2 : LANES // 2 + 1])
    wanted = (wanted == lax.broadcasted_iota(I32, (targets, tops), 1)).astype(F32)
    codes = dot(split.astype(BF16), wanted.astype(BF16), (1, 1))
    codes = (codes[0:entries, :] * 128.0 + codes[entries:, :]).astype(I32)
    source_t, kind_t = codes % tops, codes // tops

    sources = gathered.shape[0]
    chunk = min(LANES, sources)
    for first in range(0, sources, chunk):
        for n in range(first // cells_c // nx, (first + chunk) // cells_c // nx):
            for i in steps_x:
                if i:
                    sent_x[n, i].wait_recv()
        here = slice(first, first + chunk)
        place = parents(gathered[here, k : k + 1], gathered[here, k + 1 : k + 2])

        def store_t(o, m):
            count_t[here, o * targets : (o + 1) * targets] = m

        count(place, source_t, kind_t, store_t)
        turned[:, here] = gathered[here, :].T

    loads[2].wait()
    packed = dot(turned[0:k, :], count_t[:, 0:targets]).astype(BF16)
    partial = dot(m2l_v[0], packed)
    for o in range(1, kinds):
        packed = dot(turned[0:k, :], count_t[:, o * targets : (o + 1) * targets]).astype(BF16)
        partial = partial + dot(m2l_v[o], packed)
    pad_v[0:k, 0:targets] = partial
    shares[...] = pad_v[:, 0:targets].T.astype(BF16)

    sent_q = {}
    for n, (j, c) in enumerate(steps_q):
        if n:
            sent_q[n] = send(part(shares, n), part(arrived, n), sems_q, n - 1, at(-j, 0, -c, 0))

    to_before.wait_recv()
    to_after.wait_recv()
    near = jnp.zeros((k, cells_b), F32)
    for o in range(kinds):
        packed = dot(window[0:k, :], count_b[:, o * cells_b : (o + 1) * cells_b]).astype(BF16)
        near = near + dot(m2l_v[o], packed)
    pad_v[0:k, 0:cells_b] = near
    near_t[...] = pad_v[:, 0:cells_b].T
    one_hot_bt = one_hot_b.T.astype(BF16)

    top_local = shares[0:cells_c, :].astype(F32)
    for n in sent_q:
        sent_q[n].wait_recv()
    for n in sent_q:
        top_local = top_local + arrived[n * cells_c : (n + 1) * cells_c, :].astype(F32)
    top_local = top_local.astype(BF16)[:, 0:k]

    local_c = jnp.zeros((cells_c, k), F32)
    for o in range(8):
        local_c = local_c + jnp.where(octant_c == o, dot(top_local, m2m_v[o]), 0.0)
    local_c = local_c.astype(BF16)
    for o in range(8):
        prod_c[o * cells_c : (o + 1) * cells_c, :] = dot(local_c, m2m_v[o])
    full = prod_c[...]
    rounded = full.astype(BF16)
    rest = (full - rounded.astype(F32)).astype(BF16)
    far = dot(one_hot_bt, rounded) + dot(one_hot_bt, rest)
    local_b = (near_t[:, 0:k] + far).astype(BF16)
    for o in range(8):
        prod_b[o * cells_b : (o + 1) * cells_b, :] = dot(local_b, m2m_v[o]).astype(BF16)
    out_ref[...] = dot(prod_b[...], one_hot_a[...], (0, 0)).astype(BF16)

    to_before.wait_send()
    to_after.wait_send()
    for sent in (sent_z, sent_x, sent_heads, sent_q):
        for copy in sent.values():
            copy.wait_send()


def body(dims, *args):
    (
        leaf_mult,
        fine_count,
        parent_a,
        octant_a,
        parent_b,
        octant_b,
        parent_c,
        octant_c,
        list_b_src,
        list_b_off,
        list_t_src,
        list_t_off,
        m2m_ops,
        m2l_ops,
    ) = args
    ny, nz, nx = dims
    k, cells_a = leaf_mult.shape
    cells_b = parent_b.shape[0]
    cells_c = parent_c.shape[0]
    kinds = m2l_ops.shape[0]
    kp = -(-(k + 2) // LANES) * LANES
    kr = -(-k // 16) * 16
    sources = nz * nx * cells_c
    targets = ny * CORES * cells_c
    wide = max(cells_b, targets)
    vmem = pl.BlockSpec(memory_space=pltpu.VMEM)
    smem = pl.BlockSpec(memory_space=pltpu.SMEM)
    hbm = pl.BlockSpec(memory_space=pl.ANY)

    def pair(n):
        return [pltpu.SemaphoreType.DMA((n,)), pltpu.SemaphoreType.DMA((n,))]

    fine = pl.pallas_call(
        functools.partial(kernel, dims),
        out_shape=jax.ShapeDtypeStruct((k, cells_a), BF16),
        in_specs=[hbm, smem] + [vmem] * 10 + [hbm, hbm],
        out_specs=vmem,
        scratch_shapes=[
            pltpu.VMEM((k, cells_a), BF16),
            pltpu.VMEM(m2m_ops.shape, BF16),
            pltpu.VMEM(m2l_ops.shape, BF16),
            pltpu.VMEM((8 * cells_b, cells_a), BF16),
            pltpu.VMEM((k, 8 * cells_b), BF16),
            pltpu.VMEM((kr, 3 * cells_b), BF16),
            pltpu.VMEM((cells_b, kp), F32),
            pltpu.VMEM((kp, wide), F32),
            pltpu.VMEM((3 * cells_b, kinds * cells_b), BF16),
            pltpu.VMEM((sources, kinds * targets), BF16),
            pltpu.VMEM((sources, kp), BF16),
            pltpu.VMEM((kp, sources), BF16),
            pltpu.VMEM((targets, LANES), BF16),
            pltpu.VMEM((targets, kp), BF16),
            pltpu.VMEM((targets, kp), BF16),
            pltpu.VMEM((8 * cells_c, k), F32),
            pltpu.VMEM((8 * cells_b, k), BF16),
            pltpu.SemaphoreType.DMA((3,)),
            pltpu.SemaphoreType.DMA((2,)),
            pltpu.SemaphoreType.DMA((2,)),
            pair(nz - 1),
            pair(nz * (nx - 1)),
            pair(ny * CORES - 1),
            pair(ny * CORES - 1),
        ],
        compiler_params=pltpu.CompilerParams(
            collective_id=0, has_side_effects=True, vmem_limit_bytes=48 * 1024 * 1024
        ),
    )(
        leaf_mult,
        fine_count,
        parent_a.reshape(-1, LANES),
        octant_a.reshape(-1, LANES),
        parent_b.reshape(1, -1),
        octant_b.reshape(1, -1),
        parent_c.reshape(1, -1),
        octant_c.reshape(1, -1),
        list_b_src.T,
        list_b_off.T,
        list_t_src.T,
        list_t_off.T,
        m2m_ops,
        m2l_ops,
    )
    return fine


def solution(mesh):
    nx = mesh.shape["coef"]
    plane = mesh.shape["leaf"] // CORES
    nz = 1
    while nz * nz < plane:
        nz *= 2
    both = P(("leaf", "coef"))
    rows = P(("leaf", "coef"), None)
    in_specs = (P(None, ("leaf", "coef")),) + (both,) * 7 + (rows, rows) + (P(),) * 4
    return jax.shard_map(
        functools.partial(body, (plane // nz, nz, nx)),
        mesh=mesh,
        in_specs=in_specs,
        out_specs=P(None, ("leaf", "coef")),
        check_vma=False,
    )
```

time: 55 us -> 48.4 us (0.88)
  Pallas kernels: 50.4 us -> 43.7 us
    pallas_call x1, Pallas kernels: 50.4 us -> 43.7 us  [body(): pl.pallas_call(functools.partial(kernel, dims), out_shape=jax.ShapeDtypeS...]
where the time goes in v2:
time: 48.4 us; the launch traced here: 48.2 us
  Pallas kernels  43.7 us (90%)
  local copies, waits for them, and re-layouts  3.54 us (7%)
  between operations  0.95 us (2%)
    pallas_call x1, Pallas kernels, body(): pl.pallas_call(functools.partial(kernel, dims), out_shape=jax.ShapeDtypeS...  43.7 us
    unnamed x27, local copies, waits for them, and re-layouts  3.54 us

profile of v2, /device:TPU:1, one launch (start us, length us, event | category | flops | bytes accessed | tf_op | source)
XLA Modules:
  0.0 48.2 jit_solution(15846385886949985415)
XLA Ops:
  0.8 1.7 %copy.15.m2m_hbm = bf16[8,289,289]{2,1,0:T(8,128)(2,1)S(1)} copy(bf16[8,289,289]{2,0,1:T(8,128)(2,1)} %param.26) | data formatting | bytes 2672672 | tf_op args[12]
  2.5 0.0 copy-done.11
  2.5 0.0 copy-start
  2.5 0.0 copy-start.1
  2.5 0.0 copy-start.2
  2.5 0.0 copy-start.3
  2.6 0.0 copy-start.4
  2.6 0.0 copy-start.5
  2.6 0.0 copy-start.6
  2.6 0.0 copy-start.7
  2.6 0.0 copy-start.8
  2.6 0.0 copy-start.9
  2.6 0.0 copy-start.10
  2.6 0.2 copy.16.m2l_hbm
  2.9 0.7 %copy-done = bf16[289,1024]{1,0:T(8,128)(2,1)S(1)} copy-done((bf16[289,1024]{1,0:T(8,128)(2,1)S(1)}, bf16[289,1024]{1,0:T(8,128)(2,1)}, u32[]{:S(2)}) %copy-start) | copy-done | bytes 591896
  3.6 0.0 copy-done.1
  3.6 0.0 copy-done.2
  3.6 0.0 copy-done.3
  3.6 0.0 copy-done.4
  3.6 0.0 copy-done.5
  3.6 0.0 copy-done.6
  3.6 0.0 copy-done.7
  3.7 43.7 %shard_map.136 = bf16[289,1024]{1,0:T(8,128)(2,1)S(1)} custom-call(bf16[289,1024]{1,0:T(8,128)(2,1)S(1)} %copy-done, s32[1]{0:T(128)S(6)} %copy.18.count_ref, s32[8,128]{1,0:T(8,128)S(1)} %bitcast.14, s32[8,128]{1,0:T(8,128)S(1)} %bitcast.15, s32[1,128]{1,0:T(1,128)S(1)} %bitcast.16, s32[1,128]{1,0:T(1,128)S(1)} %bitcast.17, s32[1,16]{1,0:T(1,128)S(1)} %bitcast.18, ...), custom_call_target="tpu_custom_call" | custom-call | tf_op jit(solution)/shard_map/pallas_call | solution.py:350
  47.4 0.8 %copy.19 = bf16[289,1024]{1,0:T(8,128)(2,1)} copy(bf16[289,1024]{1,0:T(8,128)(2,1)S(1)} %shard_map.136) | data formatting | bytes 1183744
  (4 shorter events, 0.0 us)
Async XLA Ops:
  0.0 2.5 %copy-start.11 = (bf16[8,289,289]{2,0,1:T(8,128)(2,1)S(1)}, bf16[8,289,289]{2,0,1:T(8,128)(2,1)}, u32[]{:S(2)}) copy-start(bf16[8,289,289]{2,0,1:T(8,128)(2,1)} %param.27) | copy-start | bytes 4009012
  2.5 1.1 %copy-start = (bf16[289,1024]{1,0:T(8,128)(2,1)S(1)}, bf16[289,1024]{1,0:T(8,128)(2,1)}, u32[]{:S(2)}) copy-start(bf16[289,1024]{1,0:T(8,128)(2,1)} %leaf_hbm.1) | copy-start | bytes 1775620
  2.5 1.1 %copy-start.1 = (s32[1024,16]{0,1:T(8,128)S(1)}, s32[1024,16]{0,1:T(8,128)}, u32[]{:S(2)}) copy-start(s32[1024,16]{0,1:T(8,128)} %param.24) | copy-start | bytes 196612
  2.5 1.1 %copy-start.2 = (s32[1024,16]{0,1:T(8,128)S(1)}, s32[1024,16]{0,1:T(8,128)}, u32[]{:S(2)}) copy-start(s32[1024,16]{0,1:T(8,128)} %param.25) | copy-start | bytes 196612
  2.5 1.0 %copy-start.3 = (s32[128,16]{0,1:T(8,128)S(1)}, s32[128,16]{0,1:T(8,128)}, u32[]{:S(2)}) copy-start(s32[128,16]{0,1:T(8,128)} %param.22) | copy-start | bytes 24580
  2.6 1.0 %copy-start.4 = (s32[128,16]{0,1:T(8,128)S(1)}, s32[128,16]{0,1:T(8,128)}, u32[]{:S(2)}) copy-start(s32[128,16]{0,1:T(8,128)} %param.23) | copy-start | bytes 24580
  2.6 1.0 %copy-start.5 = (s32[1024]{0:T(1024)S(1)}, s32[1024]{0:T(1024)}, u32[]{:S(2)}) copy-start(s32[1024]{0:T(1024)} %param.16) | copy-start | bytes 12292
  2.6 1.0 %copy-start.6 = (s32[1024]{0:T(1024)S(1)}, s32[1024]{0:T(1024)}, u32[]{:S(2)}) copy-start(s32[1024]{0:T(1024)} %param.17) | copy-start | bytes 12292
  2.6 1.0 %copy-start.7 = (s32[128]{0:T(128)S(1)}, s32[128]{0:T(128)}, u32[]{:S(2)}) copy-start(s32[128]{0:T(128)} %param.18) | copy-start | bytes 1540
  2.6 1.0 %copy-start.8 = (s32[128]{0:T(128)S(1)}, s32[128]{0:T(128)}, u32[]{:S(2)}) copy-start(s32[128]{0:T(128)} %param.19) | copy-start | bytes 1540
  2.6 1.0 %copy-start.9 = (s32[16]{0:T(128)S(1)}, s32[16]{0:T(128)}, u32[]{:S(2)}) copy-start(s32[16]{0:T(128)} %param.20) | copy-start | bytes 196
  2.6 1.0 %copy-start.10 = (s32[16]{0:T(128)S(1)}, s32[16]{0:T(128)}, u32[]{:S(2)}) copy-start(s32[16]{0:T(128)} %param.21) | copy-start | bytes 196

commit v3 on v2

--- a/solution.py
+++ b/solution.py
@@ -13,6 +13,7 @@
 I32 = jnp.int32
 LANES = 128
 CORES = 2
+MAIN = 256
 
 
 def dot(a, b, contract=(1, 0)):
@@ -45,10 +46,14 @@
     m2l_hbm,
     out_ref,
     leaf_v,
+    m2m_in,
+    m2l_in,
     m2m_v,
-    m2l_v,
+    m2m_p,
+    m2l_p,
+    flat,
+    stack,
     one_hot_a,
-    grouped_v,
     window,
     near_t,
     pad_v,
@@ -75,7 +80,8 @@
     cells_b = pb_ref.shape[1]
     cells_c = pc_ref.shape[1]
     entries, tops = lts_ref.shape
-    kinds = m2l_v.shape[0]
+    kinds = m2l_in.shape[1]
+    rest, rest_pad = k - MAIN, (m2l_p.shape[1] - kinds * MAIN) // kinds
     kp = gathered.shape[1]
 
     leaf_i, x = lax.axis_index("leaf"), lax.axis_index("coef")
@@ -103,8 +109,8 @@
 
     loads = [
         pltpu.make_async_copy(leaf_hbm, leaf_v, load_sem.at[0]),
-        pltpu.make_async_copy(m2m_hbm, m2m_v, load_sem.at[1]),
-        pltpu.make_async_copy(m2l_hbm, m2l_v, load_sem.at[2]),
+        pltpu.make_async_copy(m2m_hbm, m2m_in, load_sem.at[1]),
+        pltpu.make_async_copy(m2l_hbm, m2l_in, load_sem.at[2]),
     ]
     for load in loads:
         load.start()
@@ -119,6 +125,33 @@
     for partner in partners:
         pl.semaphore_signal(barrier, inc=1, device_id=partner, device_id_type=MESH)
 
+    def rest_of(o):
+        return slice(kinds * MAIN + o * rest_pad, kinds * MAIN + o * rest_pad + rest)
+
+    def separate(operators, whole, joined):
+        for t in range(-(-k // LANES)):
+            width = min(LANES, k - t * LANES)
+            lanes = slice(t * LANES, t * LANES + width)
+            flat[t, :, 0:width] = operators[:, :, lanes].astype(F32).reshape(k * kinds, width)
+            for o in range(kinds):
+                tile = flat.at[t][pl.ds(o, k, stride=kinds), :][:, 0:width].astype(BF16)
+                if whole is not None:
+                    whole[o, :, lanes] = tile
+                first = t * LANES
+                if first < MAIN:
+                    joined[:, o * MAIN + first : o * MAIN + first + width] = tile
+                else:
+                    joined[:, rest_of(o)] = tile
+
+    def put(o, value):
+        n = value.shape[1]
+        stack[o * MAIN : (o + 1) * MAIN, 0:n] = value[0:MAIN, :]
+        stack[rest_of(o), 0:n] = value[MAIN:, :]
+
+    stack[kinds * MAIN :, :] = jnp.zeros((kinds * rest_pad, stack.shape[1]), BF16)
+    m2m_p[:, kinds * MAIN :] = jnp.zeros((k, kinds * rest_pad), BF16)
+    m2l_p[:, kinds * MAIN :] = jnp.zeros((k, kinds * rest_pad), BF16)
+
     cell = (
         lax.broadcasted_iota(I32, pa_ref.shape, 0) * LANES
         + lax.broadcasted_iota(I32, pa_ref.shape, 1)
@@ -130,28 +163,32 @@
         one_hot_a[:, r * LANES : (r + 1) * LANES] = (slot == code_a[r : r + 1, :]).astype(F32).astype(BF16)
 
     loads[0].wait()
+    loads[1].wait()
+    separate(m2m_in, m2m_v, m2m_p)
     for o in range(0, 8, 2):
-        rows = slice(o * cells_b, (o + 2) * cells_b)
-        grouped_v[:, rows] = dot(leaf_v[...], one_hot_a[rows, :], (1, 1)).astype(BF16)
-    loads[1].wait()
-    mult_b = dot(m2m_v[0], grouped_v[:, :cells_b])
-    for o in range(1, 8):
-        mult_b = mult_b + dot(m2m_v[o], grouped_v[:, o * cells_b : (o + 1) * cells_b])
-    mult_b = mult_b.astype(BF16)
+        pair = dot(leaf_v[...], one_hot_a[o * cells_b : (o + 2) * cells_b, :], (1, 1)).astype(BF16)
+        put(o, pair[:, :cells_b])
+        put(o + 1, pair[:, cells_b:])
+    mult_b = dot(m2m_p[...], stack[:, :cells_b]).astype(BF16)
     window[:, cells_b : 2 * cells_b] = jnp.zeros((window.shape[0], cells_b), BF16)
     window[0:k, cells_b : 2 * cells_b] = mult_b
 
     code_b = ob_ref[...] * cells_c + pb_ref[...] - device * cells_c
     slots_b = 8 * cells_c
     one_hot_b = (lax.broadcasted_iota(I32, (slots_b, cells_b), 0) == code_b).astype(F32)
-    grouped_c = dot(mult_b, one_hot_b.astype(BF16), (1, 1)).astype(BF16)
-    mult_c = dot(m2m_v[0], grouped_c[:, :cells_c])
-    for o in range(1, 8):
-        mult_c = mult_c + dot(m2m_v[o], grouped_c[:, o * cells_c : (o + 1) * cells_c])
+    grouped_c = dot(mult_b, one_hot_b.astype(BF16), (1, 1))
+    octant_of = lax.broadcasted_iota(I32, (1, slots_b), 1) // cells_c
+    for o in range(8):
+        put(o, jnp.where(octant_of == o, grouped_c, 0.0).astype(BF16))
+    mult_c = dot(m2m_p[...], stack[:, 0:slots_b])
+    turn = slots_b // 2
+    while turn >= cells_c:
+        mult_c = mult_c + pltpu.roll(mult_c, turn, 1)
+        turn //= 2
     octant_c = oc_ref[...]
-    shifted = jnp.zeros((k, cells_c), F32)
     for o in range(8):
-        shifted = shifted + dot(m2m_v[o], jnp.where(octant_c == o, mult_c, 0.0).astype(BF16))
+        put(o, jnp.where(octant_c == o, mult_c[:, 0:cells_c], 0.0).astype(BF16))
+    shifted = dot(m2m_p[...], stack[:, 0:cells_c])
     pad_v[...] = jnp.zeros(pad_v.shape, F32)
     pad_v[0:k, 0:cells_c] = shifted
     shifted_t = pad_v[:, 0:LANES].T[0:cells_c, :]
@@ -225,6 +262,9 @@
     place_b = lax.broadcasted_iota(I32, (3 * cells_b, cells_b), 0)
     count(place_b, lbs_ref[...] - (device - 1) * cells_b, lbo_ref[...], store_b)
 
+    loads[2].wait()
+    separate(m2l_in, None, m2l_p)
+
     for n in range(1, nz):
         sent_z[n].wait_recv()
         spread(n)
@@ -260,12 +300,9 @@
         count(place, source_t, kind_t, store_t)
         turned[:, here] = gathered[here, :].T
 
-    loads[2].wait()
-    packed = dot(turned[0:k, :], count_t[:, 0:targets]).astype(BF16)
-    partial = dot(m2l_v[0], packed)
-    for o in range(1, kinds):
-        packed = dot(turned[0:k, :], count_t[:, o * targets : (o + 1) * targets]).astype(BF16)
-        partial = partial + dot(m2l_v[o], packed)
+    for o in range(kinds):
+        put(o, dot(turned[0:k, :], count_t[:, o * targets : (o + 1) * targets]).astype(BF16))
+    partial = dot(m2l_p[...], stack[:, 0:targets])
     pad_v[0:k, 0:targets] = partial
     shares[...] = pad_v[:, 0:targets].T.astype(BF16)
 
@@ -276,10 +313,9 @@
 
     to_before.wait_recv()
     to_after.wait_recv()
-    near = jnp.zeros((k, cells_b), F32)
     for o in range(kinds):
-        packed = dot(window[0:k, :], count_b[:, o * cells_b : (o + 1) * cells_b]).astype(BF16)
-        near = near + dot(m2l_v[o], packed)
+        put(o, dot(window[0:k, :], count_b[:, o * cells_b : (o + 1) * cells_b]).astype(BF16))
+    near = dot(m2l_p[...], stack[:, 0:cells_b])
     pad_v[0:k, 0:cells_b] = near
     near_t[...] = pad_v[:, 0:cells_b].T
     one_hot_bt = one_hot_b.T.astype(BF16)
@@ -340,6 +376,7 @@
     sources = nz * nx * cells_c
     targets = ny * CORES * cells_c
     wide = max(cells_b, targets)
+    stacked = kinds * (MAIN + -(-(k - MAIN) // 16) * 16)
     vmem = pl.BlockSpec(memory_space=pltpu.VMEM)
     smem = pl.BlockSpec(memory_space=pltpu.SMEM)
     hbm = pl.BlockSpec(memory_space=pl.ANY)
@@ -354,10 +391,14 @@
         out_specs=vmem,
         scratch_shapes=[
             pltpu.VMEM((k, cells_a), BF16),
-            pltpu.VMEM(m2m_ops.shape, BF16),
-            pltpu.VMEM(m2l_ops.shape, BF16),
+            pltpu.VMEM((k, 8, k), BF16),
+            pltpu.VMEM((k, kinds, k), BF16),
+            pltpu.VMEM((8, k, k), BF16),
+            pltpu.VMEM((k, stacked), BF16),
+            pltpu.VMEM((k, stacked), BF16),
+            pltpu.VMEM((-(-k // LANES), kinds * k, LANES), F32),
+            pltpu.VMEM((stacked, wide), BF16),
             pltpu.VMEM((8 * cells_b, cells_a), BF16),
-            pltpu.VMEM((k, 8 * cells_b), BF16),
             pltpu.VMEM((kr, 3 * cells_b), BF16),
             pltpu.VMEM((cells_b, kp), F32),
             pltpu.VMEM((kp, wide), F32),
@@ -379,7 +420,7 @@
             pair(ny * CORES - 1),
         ],
         compiler_params=pltpu.CompilerParams(
-            collective_id=0, has_side_effects=True, vmem_limit_bytes=48 * 1024 * 1024
+            collective_id=0, has_side_effects=True, vmem_limit_bytes=56 * 1024 * 1024
         ),
     )(
         leaf_mult,
@@ -394,8 +435,8 @@
         list_b_off.T,
         list_t_src.T,
         list_t_off.T,
-        m2m_ops,
-        m2l_ops,
+        m2m_ops.transpose(1, 0, 2),
+        m2l_ops.transpose(1, 0, 2),
     )
     return fine
 

time: 48.4 us -> 46.2 us (0.955)
  local copies, waits for them, and re-layouts: 3.54 us -> 1.93 us
    unnamed x27 -> x1, local copies, waits for them, and re-layouts: 3.54 us -> 1.93 us
where the time goes in v3:
time: 46.2 us; the launch traced here: 46 us
  Pallas kernels  43.4 us (94%)
  local copies, waits for them, and re-layouts  1.93 us (4%)
  between operations  0.66 us (1%)
    pallas_call x1, Pallas kernels, body(): pl.pallas_call(functools.partial(kernel, dims), out_shape=jax.ShapeDtypeS...  43.4 us
    unnamed x1, local copies, waits for them, and re-layouts  1.93 us

profile of v3, /device:TPU:1, one launch (start us, length us, event | category | flops | bytes accessed | tf_op | source)
XLA Modules:
  0.0 46.0 jit_solution(1664173235149732406)
XLA Ops:
  0.7 43.4 %shard_map.136 = bf16[289,1024]{1,0:T(8,128)(2,1)} custom-call(bf16[289,1024]{1,0:T(8,128)(2,1)} %leaf_hbm.1, s32[1]{0:T(128)S(6)} %copy.16.count_ref, s32[8,128]{1,0:T(8,128)} %bitcast.18, s32[8,128]{1,0:T(8,128)} %bitcast.19, s32[1,128]{1,0:T(1,128)} %bitcast.20, s32[1,128]{1,0:T(1,128)} %bitcast.21, s32[1,16]{1,0:T(1,128)} %bitcast.22, s32[1,16]{1,0:T(1,128)} %bitcast.23, ...), custom_call_target="tpu_custom_call" | custom-call | tf_op jit(solution)/shard_map/pallas_call | solution.py:387
  44.0 1.9 %copy.17 = bf16[289,1024]{1,0:T(8,128)(2,1)} copy(bf16[289,1024]{1,0:T(8,128)(2,1)} %shard_map.136) | data formatting | bytes 1183744

commit v4 on v3

--- a/solution.py
+++ b/solution.py
@@ -30,7 +30,7 @@
 
 def kernel(
     dims,
-    leaf_hbm,
+    leaf_ref,
     count_ref,
     pa_ref,
     oa_ref,
@@ -45,10 +45,10 @@
     m2m_hbm,
     m2l_hbm,
     out_ref,
-    leaf_v,
     m2m_in,
     m2l_in,
     m2m_v,
+    m2m_t,
     m2m_p,
     m2l_p,
     flat,
@@ -61,6 +61,7 @@
     count_t,
     gathered,
     turned,
+    early,
     heads,
     shares,
     arrived,
@@ -75,8 +76,7 @@
     sems_q,
 ):
     ny, nz, nx = dims
-    k = leaf_v.shape[0]
-    cells_a = leaf_v.shape[1]
+    k, cells_a = leaf_ref.shape
     cells_b = pb_ref.shape[1]
     cells_c = pc_ref.shape[1]
     entries, tops = lts_ref.shape
@@ -108,9 +108,8 @@
     after = linear(lax.rem(device + 1, devices))
 
     loads = [
-        pltpu.make_async_copy(leaf_hbm, leaf_v, load_sem.at[0]),
-        pltpu.make_async_copy(m2m_hbm, m2m_in, load_sem.at[1]),
-        pltpu.make_async_copy(m2l_hbm, m2l_in, load_sem.at[2]),
+        pltpu.make_async_copy(m2m_hbm, m2m_in, load_sem.at[0]),
+        pltpu.make_async_copy(m2l_hbm, m2l_in, load_sem.at[1]),
     ]
     for load in loads:
         load.start()
@@ -163,10 +162,11 @@
         one_hot_a[:, r * LANES : (r + 1) * LANES] = (slot == code_a[r : r + 1, :]).astype(F32).astype(BF16)
 
     loads[0].wait()
-    loads[1].wait()
     separate(m2m_in, m2m_v, m2m_p)
+    for o in range(8):
+        m2m_t[o] = m2m_v[o].T
     for o in range(0, 8, 2):
-        pair = dot(leaf_v[...], one_hot_a[o * cells_b : (o + 2) * cells_b, :], (1, 1)).astype(BF16)
+        pair = dot(leaf_ref[...], one_hot_a[o * cells_b : (o + 2) * cells_b, :], (1, 1)).astype(BF16)
         put(o, pair[:, :cells_b])
         put(o + 1, pair[:, cells_b:])
     mult_b = dot(m2m_p[...], stack[:, :cells_b]).astype(BF16)
@@ -176,28 +176,21 @@
     code_b = ob_ref[...] * cells_c + pb_ref[...] - device * cells_c
     slots_b = 8 * cells_c
     one_hot_b = (lax.broadcasted_iota(I32, (slots_b, cells_b), 0) == code_b).astype(F32)
-    grouped_c = dot(mult_b, one_hot_b.astype(BF16), (1, 1))
-    octant_of = lax.broadcasted_iota(I32, (1, slots_b), 1) // cells_c
+    grouped_c = dot(one_hot_b.astype(BF16), mult_b, (1, 1)).astype(BF16)
+    mult_c = dot(grouped_c[0:cells_c, :], m2m_t[0])
+    for o in range(1, 8):
+        mult_c = mult_c + dot(grouped_c[o * cells_c : (o + 1) * cells_c, :], m2m_t[o])
+    octant_c = column_of(oc_ref[...])
+    shifted = jnp.zeros((cells_c, k), F32)
     for o in range(8):
-        put(o, jnp.where(octant_of == o, grouped_c, 0.0).astype(BF16))
-    mult_c = dot(m2m_p[...], stack[:, 0:slots_b])
-    turn = slots_b // 2
-    while turn >= cells_c:
-        mult_c = mult_c + pltpu.roll(mult_c, turn, 1)
-        turn //= 2
-    octant_c = oc_ref[...]
-    for o in range(8):
-        put(o, jnp.where(octant_c == o, mult_c[:, 0:cells_c], 0.0).astype(BF16))
-    shifted = dot(m2m_p[...], stack[:, 0:cells_c])
-    pad_v[...] = jnp.zeros(pad_v.shape, F32)
-    pad_v[0:k, 0:cells_c] = shifted
-    shifted_t = pad_v[:, 0:LANES].T[0:cells_c, :]
+        shifted = shifted + dot(jnp.where(octant_c == o, mult_c, 0.0).astype(BF16), m2m_t[o])
+    pad_v[0:cells_c, :] = jnp.zeros((cells_c, pad_v.shape[1]), F32)
+    pad_v[0:cells_c, 0:k] = shifted
     parent_c = column_of(pc_ref[...])
-    octant_c = column_of(octant_c)
     high = (parent_c // 32).astype(F32)
     low = (parent_c % 32).astype(F32)
     lane = lax.broadcasted_iota(I32, (cells_c, kp), 1)
-    message = jnp.where(lane == k, high, jnp.where(lane == k + 1, low, shifted_t))
+    message = jnp.where(lane == k, high, jnp.where(lane == k + 1, low, pad_v[0:cells_c, 0:kp]))
     gathered[0:cells_c, :] = message.astype(BF16)
     lane = lax.broadcasted_iota(I32, (cells_c, LANES), 1)
     heads[0:cells_c, :] = jnp.where(lane < LANES // 2, high, low).astype(BF16)
@@ -237,11 +230,6 @@
     for n, (j, c) in enumerate(steps_q):
         if n:
             sent_heads[n] = send(part(heads, 0), part(heads, n), sems_h, n - 1, at(j, 0, c, 0))
-    mine = window.at[:, cells_b : 2 * cells_b]
-    near_sems = (near_send, near_recv)
-    to_before = send(mine, window.at[:, 2 * cells_b : 3 * cells_b], near_sems, 0, before)
-    to_after = send(mine, window.at[:, 0:cells_b], near_sems, 1, after)
-
     def count(place, wanted, kind, store):
         weights = []
         for first in range(0, kinds, 4):
@@ -262,12 +250,17 @@
     place_b = lax.broadcasted_iota(I32, (3 * cells_b, cells_b), 0)
     count(place_b, lbs_ref[...] - (device - 1) * cells_b, lbo_ref[...], store_b)
 
-    loads[2].wait()
+    loads[1].wait()
     separate(m2l_in, None, m2l_p)
 
     for n in range(1, nz):
         sent_z[n].wait_recv()
         spread(n)
+
+    mine = window.at[:, cells_b : 2 * cells_b]
+    near_sems = (near_send, near_recv)
+    to_before = send(mine, window.at[:, 2 * cells_b : 3 * cells_b], near_sems, 0, before)
+    to_after = send(mine, window.at[:, 0:cells_b], near_sems, 1, after)
 
     for n in sent_heads:
         sent_heads[n].wait_recv()
@@ -285,7 +278,8 @@
     source_t, kind_t = codes % tops, codes // tops
 
     sources = gathered.shape[0]
-    chunk = min(LANES, sources)
+    half = sources // 2
+    chunk = min(LANES, half)
     for first in range(0, sources, chunk):
         for n in range(first // cells_c // nx, (first + chunk) // cells_c // nx):
             for i in steps_x:
@@ -299,9 +293,14 @@
 
         count(place, source_t, kind_t, store_t)
         turned[:, here] = gathered[here, :].T
+        if first + chunk == half:
+            for o in range(kinds):
+                lanes = slice(o * targets, (o + 1) * targets)
+                early[:, lanes] = dot(turned[0:k, 0:half], count_t[0:half, lanes])
 
     for o in range(kinds):
-        put(o, dot(turned[0:k, :], count_t[:, o * targets : (o + 1) * targets]).astype(BF16))
+        lanes = slice(o * targets, (o + 1) * targets)
+        put(o, (early[:, lanes] + dot(turned[0:k, half:], count_t[half:, lanes])).astype(BF16))
     partial = dot(m2l_p[...], stack[:, 0:targets])
     pad_v[0:k, 0:targets] = partial
     shares[...] = pad_v[:, 0:targets].T.astype(BF16)
@@ -313,8 +312,10 @@
 
     to_before.wait_recv()
     to_after.wait_recv()
-    for o in range(kinds):
-        put(o, dot(window[0:k, :], count_b[:, o * cells_b : (o + 1) * cells_b]).astype(BF16))
+    for o in range(0, kinds, 2):
+        pair = dot(window[0:k, :], count_b[:, o * cells_b : (o + 2) * cells_b]).astype(BF16)
+        put(o, pair[:, :cells_b])
+        put(o + 1, pair[:, cells_b:])
     near = dot(m2l_p[...], stack[:, 0:cells_b])
     pad_v[0:k, 0:cells_b] = near
     near_t[...] = pad_v[:, 0:cells_b].T
@@ -387,12 +388,12 @@
     fine = pl.pallas_call(
         functools.partial(kernel, dims),
         out_shape=jax.ShapeDtypeStruct((k, cells_a), BF16),
-        in_specs=[hbm, smem] + [vmem] * 10 + [hbm, hbm],
+        in_specs=[vmem, smem] + [vmem] * 10 + [hbm, hbm],
         out_specs=vmem,
         scratch_shapes=[
-            pltpu.VMEM((k, cells_a), BF16),
             pltpu.VMEM((k, 8, k), BF16),
             pltpu.VMEM((k, kinds, k), BF16),
+            pltpu.VMEM((8, k, k), BF16),
             pltpu.VMEM((8, k, k), BF16),
             pltpu.VMEM((k, stacked), BF16),
             pltpu.VMEM((k, stacked), BF16),
@@ -401,17 +402,18 @@
             pltpu.VMEM((8 * cells_b, cells_a), BF16),
             pltpu.VMEM((kr, 3 * cells_b), BF16),
             pltpu.VMEM((cells_b, kp), F32),
-            pltpu.VMEM((kp, wide), F32),
+            pltpu.VMEM((kp, max(kp, wide)), F32),
             pltpu.VMEM((3 * cells_b, kinds * cells_b), BF16),
             pltpu.VMEM((sources, kinds * targets), BF16),
             pltpu.VMEM((sources, kp), BF16),
             pltpu.VMEM((kp, sources), BF16),
+            pltpu.VMEM((k, kinds * targets), F32),
             pltpu.VMEM((targets, LANES), BF16),
             pltpu.VMEM((targets, kp), BF16),
             pltpu.VMEM((targets, kp), BF16),
             pltpu.VMEM((8 * cells_c, k), F32),
             pltpu.VMEM((8 * cells_b, k), BF16),
-            pltpu.SemaphoreType.DMA((3,)),
+            pltpu.SemaphoreType.DMA((2,)),
             pltpu.SemaphoreType.DMA((2,)),
             pltpu.SemaphoreType.DMA((2,)),
             pair(nz - 1),
@@ -420,7 +422,7 @@
             pair(ny * CORES - 1),
         ],
         compiler_params=pltpu.CompilerParams(
-            collective_id=0, has_side_effects=True, vmem_limit_bytes=56 * 1024 * 1024
+            collective_id=0, has_side_effects=True, vmem_limit_bytes=52 * 1024 * 1024
         ),
     )(
         leaf_mult,

time: 46.2 us -> 50.5 us (1.093)
  local copies, waits for them, and re-layouts: 1.93 us -> 8.95 us
  Pallas kernels: 43.4 us -> 40.5 us
    unnamed x1 -> x23, local copies, waits for them, and re-layouts: 1.93 us -> 8.95 us
    pallas_call x1, Pallas kernels: 43.4 us -> 40.5 us  [body(): pl.pallas_call(functools.partial(kernel, dims), out_shape=jax.ShapeDtypeS...]
where the time goes in v4:
time: 50.5 us; the launch traced here: 50.1 us
  Pallas kernels  40.5 us (80%)
  local copies, waits for them, and re-layouts  8.95 us (18%)
  between operations  0.68 us (1%)
    pallas_call x1, Pallas kernels, body(): pl.pallas_call(functools.partial(kernel, dims), out_shape=jax.ShapeDtypeS...  40.5 us
    unnamed x23, local copies, waits for them, and re-layouts  8.95 us

profile of v4, /device:TPU:1, one launch (start us, length us, event | category | flops | bytes accessed | tf_op | source)
XLA Modules:
  0.0 50.1 jit_solution(16223148041544861933)
XLA Ops:
  0.7 0.0 copy-start
  0.7 1.1 %copy-done = bf16[289,1024]{1,0:T(8,128)(2,1)S(1)} copy-done((bf16[289,1024]{1,0:T(8,128)(2,1)S(1)}, bf16[289,1024]{1,0:T(8,128)(2,1)}, u32[]{:S(2)}) %copy-start) | copy-done | bytes 591896
  1.7 0.0 copy-start.1
  1.7 0.8 %copy-done.1 = s32[1024,16]{0,1:T(8,128)S(1)} copy-done((s32[1024,16]{0,1:T(8,128)S(1)}, s32[1024,16]{0,1:T(8,128)}, u32[]{:S(2)}) %copy-start.1) | copy-done | bytes 65560
  2.6 0.0 copy-start.2
  2.6 0.8 %copy-done.2 = s32[1024,16]{0,1:T(8,128)S(1)} copy-done((s32[1024,16]{0,1:T(8,128)S(1)}, s32[1024,16]{0,1:T(8,128)}, u32[]{:S(2)}) %copy-start.2) | copy-done | bytes 65560
  3.4 0.0 copy-start.3
  3.4 0.7 %copy-done.3 = s32[128,16]{0,1:T(8,128)S(1)} copy-done((s32[128,16]{0,1:T(8,128)S(1)}, s32[128,16]{0,1:T(8,128)}, u32[]{:S(2)}) %copy-start.3) | copy-done | bytes 8216
  4.1 0.0 copy-start.4
  4.1 0.7 %copy-done.4 = s32[128,16]{0,1:T(8,128)S(1)} copy-done((s32[128,16]{0,1:T(8,128)S(1)}, s32[128,16]{0,1:T(8,128)}, u32[]{:S(2)}) %copy-start.4) | copy-done | bytes 8216
  4.8 0.0 copy-start.5
  4.8 0.7 %copy-done.5 = s32[1024]{0:T(1024)S(1)} copy-done((s32[1024]{0:T(1024)S(1)}, s32[1024]{0:T(1024)}, u32[]{:S(2)}) %copy-start.5) | copy-done | bytes 4120
  5.5 0.0 copy-start.6
  5.5 0.7 %copy-done.6 = s32[1024]{0:T(1024)S(1)} copy-done((s32[1024]{0:T(1024)S(1)}, s32[1024]{0:T(1024)}, u32[]{:S(2)}) %copy-start.6) | copy-done | bytes 4120
  6.2 0.0 copy-start.7
  6.2 0.7 %copy-done.7 = s32[128]{0:T(128)S(1)} copy-done((s32[128]{0:T(128)S(1)}, s32[128]{0:T(128)}, u32[]{:S(2)}) %copy-start.7) | copy-done | bytes 536
  6.8 0.0 copy-start.8
  6.8 0.7 %copy-done.8 = s32[128]{0:T(128)S(1)} copy-done((s32[128]{0:T(128)S(1)}, s32[128]{0:T(128)}, u32[]{:S(2)}) %copy-start.8) | copy-done | bytes 536
  7.5 0.0 copy-start.9
  7.5 0.7 %copy-done.9 = s32[16]{0:T(128)S(1)} copy-done((s32[16]{0:T(128)S(1)}, s32[16]{0:T(128)}, u32[]{:S(2)}) %copy-start.9) | copy-done | bytes 88
  8.1 0.0 copy-start.10
  8.1 0.7 %copy-done.10 = s32[16]{0:T(128)S(1)} copy-done((s32[16]{0:T(128)S(1)}, s32[16]{0:T(128)}, u32[]{:S(2)}) %copy-start.10) | copy-done | bytes 88
  8.8 40.5 %shard_map.136 = bf16[289,1024]{1,0:T(8,128)(2,1)S(1)} custom-call(bf16[289,1024]{1,0:T(8,128)(2,1)S(1)} %copy-done, s32[1]{0:T(128)S(6)} %copy.16.count_ref, s32[8,128]{1,0:T(8,128)S(1)} %bitcast.16, s32[8,128]{1,0:T(8,128)S(1)} %bitcast.17, s32[1,128]{1,0:T(1,128)S(1)} %bitcast.18, s32[1,128]{1,0:T(1,128)S(1)} %bitcast.19, s32[1,16]{1,0:T(1,128)S(1)} %bitcast.20, ...), custom_call_target="tpu_custom_call" | custom-call | tf_op jit(solution)/shard_map/pallas_call | solution.py:388
  49.3 0.8 %copy.17 = bf16[289,1024]{1,0:T(8,128)(2,1)} copy(bf16[289,1024]{1,0:T(8,128)(2,1)S(1)} %shard_map.136) | data formatting | bytes 1183744
Async XLA Ops:
  0.7 1.1 %copy-start = (bf16[289,1024]{1,0:T(8,128)(2,1)S(1)}, bf16[289,1024]{1,0:T(8,128)(2,1)}, u32[]{:S(2)}) copy-start(bf16[289,1024]{1,0:T(8,128)(2,1)} %leaf_ref.1) | copy-start | bytes 1775620
  1.7 0.8 %copy-start.1 = (s32[1024,16]{0,1:T(8,128)S(1)}, s32[1024,16]{0,1:T(8,128)}, u32[]{:S(2)}) copy-start(s32[1024,16]{0,1:T(8,128)} %param.24) | copy-start | bytes 196612
  2.6 0.8 %copy-start.2 = (s32[1024,16]{0,1:T(8,128)S(1)}, s32[1024,16]{0,1:T(8,128)}, u32[]{:S(2)}) copy-start(s32[1024,16]{0,1:T(8,128)} %param.25) | copy-start | bytes 196612
  3.4 0.7 %copy-start.3 = (s32[128,16]{0,1:T(8,128)S(1)}, s32[128,16]{0,1:T(8,128)}, u32[]{:S(2)}) copy-start(s32[128,16]{0,1:T(8,128)} %param.22) | copy-start | bytes 24580
  4.1 0.7 %copy-start.4 = (s32[128,16]{0,1:T(8,128)S(1)}, s32[128,16]{0,1:T(8,128)}, u32[]{:S(2)}) copy-start(s32[128,16]{0,1:T(8,128)} %param.23) | copy-start | bytes 24580
  4.8 0.7 %copy-start.5 = (s32[1024]{0:T(1024)S(1)}, s32[1024]{0:T(1024)}, u32[]{:S(2)}) copy-start(s32[1024]{0:T(1024)} %param.16) | copy-start | bytes 12292
  5.5 0.7 %copy-start.6 = (s32[1024]{0:T(1024)S(1)}, s32[1024]{0:T(1024)}, u32[]{:S(2)}) copy-start(s32[1024]{0:T(1024)} %param.17) | copy-start | bytes 12292
  6.2 0.7 %copy-start.7 = (s32[128]{0:T(128)S(1)}, s32[128]{0:T(128)}, u32[]{:S(2)}) copy-start(s32[128]{0:T(128)} %param.18) | copy-start | bytes 1540
  6.8 0.7 %copy-start.8 = (s32[128]{0:T(128)S(1)}, s32[128]{0:T(128)}, u32[]{:S(2)}) copy-start(s32[128]{0:T(128)} %param.19) | copy-start | bytes 1540
  7.5 0.7 %copy-start.9 = (s32[16]{0:T(128)S(1)}, s32[16]{0:T(128)}, u32[]{:S(2)}) copy-start(s32[16]{0:T(128)} %param.20) | copy-start | bytes 196
  8.1 0.7 %copy-start.10 = (s32[16]{0:T(128)S(1)}, s32[16]{0:T(128)}, u32[]{:S(2)}) copy-start(s32[16]{0:T(128)} %param.21) | copy-start | bytes 196

commit v5 on v4

--- a/solution.py
+++ b/solution.py
@@ -30,7 +30,7 @@
 
 def kernel(
     dims,
-    leaf_ref,
+    leaf_hbm,
     count_ref,
     pa_ref,
     oa_ref,
@@ -45,6 +45,7 @@
     m2m_hbm,
     m2l_hbm,
     out_ref,
+    leaf_ref,
     m2m_in,
     m2l_in,
     m2m_v,
@@ -108,6 +109,7 @@
     after = linear(lax.rem(device + 1, devices))
 
     loads = [
+        pltpu.make_async_copy(leaf_hbm, leaf_ref, load_sem.at[2]),
         pltpu.make_async_copy(m2m_hbm, m2m_in, load_sem.at[0]),
         pltpu.make_async_copy(m2l_hbm, m2l_in, load_sem.at[1]),
     ]
@@ -156,12 +158,13 @@
         + lax.broadcasted_iota(I32, pa_ref.shape, 1)
     )
     code_a = oa_ref[...] * cells_b + pa_ref[...] - device * cells_b
-    code_a = jnp.where(cell < count_ref[0], code_a, -1)
+    code_a = jnp.where(cell < count_ref[...], code_a, -1)
     slot = lax.broadcasted_iota(I32, (8 * cells_b, LANES), 0)
     for r in range(cells_a // LANES):
         one_hot_a[:, r * LANES : (r + 1) * LANES] = (slot == code_a[r : r + 1, :]).astype(F32).astype(BF16)
 
     loads[0].wait()
+    loads[1].wait()
     separate(m2m_in, m2m_v, m2m_p)
     for o in range(8):
         m2m_t[o] = m2m_v[o].T
@@ -250,7 +253,7 @@
     place_b = lax.broadcasted_iota(I32, (3 * cells_b, cells_b), 0)
     count(place_b, lbs_ref[...] - (device - 1) * cells_b, lbo_ref[...], store_b)
 
-    loads[1].wait()
+    loads[2].wait()
     separate(m2l_in, None, m2l_p)
 
     for n in range(1, nz):
@@ -379,18 +382,21 @@
     wide = max(cells_b, targets)
     stacked = kinds * (MAIN + -(-(k - MAIN) // 16) * 16)
     vmem = pl.BlockSpec(memory_space=pltpu.VMEM)
-    smem = pl.BlockSpec(memory_space=pltpu.SMEM)
     hbm = pl.BlockSpec(memory_space=pl.ANY)
+
+    def here(array):
+        return pltpu.with_memory_space_constraint(array, pltpu.HBM)
 
     def pair(n):
         return [pltpu.SemaphoreType.DMA((n,)), pltpu.SemaphoreType.DMA((n,))]
 
     fine = pl.pallas_call(
         functools.partial(kernel, dims),
-        out_shape=jax.ShapeDtypeStruct((k, cells_a), BF16),
-        in_specs=[vmem, smem] + [vmem] * 10 + [hbm, hbm],
+        out_shape=pltpu.VMEM((k, cells_a), BF16),
+        in_specs=[hbm] + [vmem] * 11 + [hbm, hbm],
         out_specs=vmem,
         scratch_shapes=[
+            pltpu.VMEM((k, cells_a), BF16),
             pltpu.VMEM((k, 8, k), BF16),
             pltpu.VMEM((k, kinds, k), BF16),
             pltpu.VMEM((8, k, k), BF16),
@@ -413,7 +419,7 @@
             pltpu.VMEM((targets, kp), BF16),
             pltpu.VMEM((8 * cells_c, k), F32),
             pltpu.VMEM((8 * cells_b, k), BF16),
-            pltpu.SemaphoreType.DMA((2,)),
+            pltpu.SemaphoreType.DMA((3,)),
             pltpu.SemaphoreType.DMA((2,)),
             pltpu.SemaphoreType.DMA((2,)),
             pair(nz - 1),
@@ -425,20 +431,20 @@
             collective_id=0, has_side_effects=True, vmem_limit_bytes=52 * 1024 * 1024
         ),
     )(
-        leaf_mult,
-        fine_count,
-        parent_a.reshape(-1, LANES),
-        octant_a.reshape(-1, LANES),
-        parent_b.reshape(1, -1),
-        octant_b.reshape(1, -1),
-        parent_c.reshape(1, -1),
-        octant_c.reshape(1, -1),
-        list_b_src.T,
-        list_b_off.T,
-        list_t_src.T,
-        list_t_off.T,
-        m2m_ops.transpose(1, 0, 2),
-        m2l_ops.transpose(1, 0, 2),
+        here(leaf_mult),
+        fine_count.reshape(1, 1),
+        here(parent_a.reshape(-1, LANES)),
+        here(octant_a.reshape(-1, LANES)),
+        here(parent_b.reshape(1, -1)),
+        here(octant_b.reshape(1, -1)),
+        here(parent_c.reshape(1, -1)),
+        here(octant_c.reshape(1, -1)),
+        here(list_b_src.T),
+        here(list_b_off.T),
+        here(list_t_src.T),
+        here(list_t_off.T),
+        here(m2m_ops.transpose(1, 0, 2)),
+        here(m2l_ops.transpose(1, 0, 2)),
     )
     return fine
 

time: 50.5 us -> 43.3 us (0.86)
  local copies, waits for them, and re-layouts: 8.95 us -> 0.82 us
  Pallas kernels: 40.5 us -> 41.7 us
    unnamed x23 -> x1, local copies, waits for them, and re-layouts: 8.95 us -> 0.82 us
    pallas_call x1, Pallas kernels: 40.5 us -> 41.7 us  [body(): pl.pallas_call(functools.partial(kernel, dims), out_shape=pltpu.VMEM((k,...]
where the time goes in v5:
time: 43.3 us; the launch traced here: 43.2 us
  Pallas kernels  41.7 us (96%)
  local copies, waits for them, and re-layouts  0.82 us (2%)
  between operations  0.66 us (2%)
    pallas_call x1, Pallas kernels, body(): pl.pallas_call(functools.partial(kernel, dims), out_shape=pltpu.VMEM((k,...  41.7 us

profile of v5, /device:TPU:1, one launch (start us, length us, event | category | flops | bytes accessed | tf_op | source)
XLA Modules:
  0.0 43.2 jit_solution(3378454416108707483)
XLA Ops:
  0.7 41.7 %shard_map.136 = bf16[289,1024]{1,0:T(8,128)(2,1)S(1)} custom-call(bf16[289,1024]{1,0:T(8,128)(2,1)} %leaf_hbm.1, s32[1,1]{1,0:T(1,128)} %bitcast.13.count_ref, s32[8,128]{1,0:T(8,128)} %bitcast.20, s32[8,128]{1,0:T(8,128)} %bitcast.21, s32[1,128]{1,0:T(1,128)} %bitcast.22, s32[1,128]{1,0:T(1,128)} %bitcast.23, s32[1,16]{1,0:T(1,128)} %bitcast.24, ...), custom_call_target="tpu_custom_call" | custom-call | tf_op jit(solution)/shard_map/pallas_call | solution.py:393
  42.3 0.8 %copy.16 = bf16[289,1024]{1,0:T(8,128)(2,1)} copy(bf16[289,1024]{1,0:T(8,128)(2,1)S(1)} %shard_map.136) | data formatting | bytes 1183744

commit v6 on v5

--- a/solution.py
+++ b/solution.py
@@ -22,6 +22,11 @@
     )
 
 
+def stacked_dot(operator, stack):
+    cut = operator.shape[0] // 32 * 16
+    return jnp.concatenate([dot(operator[0:cut, :], stack), dot(operator[cut:, :], stack)], axis=0)
+
+
 def column_of(row):
     n = row.shape[1]
     diagonal = lax.broadcasted_iota(I32, (n, n), 0) == lax.broadcasted_iota(I32, (n, n), 1)
@@ -32,6 +37,19 @@
     dims,
     leaf_hbm,
     count_ref,
+    pa_hbm,
+    oa_hbm,
+    pb_hbm,
+    ob_hbm,
+    pc_hbm,
+    oc_hbm,
+    lbs_hbm,
+    lbo_hbm,
+    lts_hbm,
+    lto_hbm,
+    m2m_hbm,
+    m2l_hbm,
+    out_ref,
     pa_ref,
     oa_ref,
     pb_ref,
@@ -42,9 +60,6 @@
     lbo_ref,
     lts_ref,
     lto_ref,
-    m2m_hbm,
-    m2l_hbm,
-    out_ref,
     leaf_ref,
     m2m_in,
     m2l_in,
@@ -102,6 +117,7 @@
 
     steps_z = sorted(range(nz), key=lambda i: (min(i, nz - i), i))
     steps_x = range(nx)
+    direct = [n for n, j in enumerate(steps_z) if min(j, nz - j) == 1]
     steps_q = sorted(
         [(i, c) for i in range(ny) for c in range(CORES)], key=lambda s: (min(s[0], ny - s[0]), s)
     )
@@ -113,18 +129,36 @@
         pltpu.make_async_copy(m2m_hbm, m2m_in, load_sem.at[0]),
         pltpu.make_async_copy(m2l_hbm, m2l_in, load_sem.at[1]),
     ]
-    for load in loads:
+    index_refs = (
+        (pa_hbm, pa_ref),
+        (oa_hbm, oa_ref),
+        (pb_hbm, pb_ref),
+        (ob_hbm, ob_ref),
+        (pc_hbm, pc_ref),
+        (oc_hbm, oc_ref),
+        (lbs_hbm, lbs_ref),
+        (lbo_hbm, lbo_ref),
+        (lts_hbm, lts_ref),
+        (lto_hbm, lto_ref),
+    )
+    indices = [
+        pltpu.make_async_copy(src, dst, load_sem.at[3 + i]) for i, (src, dst) in enumerate(index_refs)
+    ]
+    for load in indices[0:2] + loads[0:2]:
         load.start()
 
     barrier = pltpu.get_barrier_semaphore()
     partners = (
         [at(0, j, 0, 0) for j in steps_z if j]
         + [at(0, 0, 0, i) for i in steps_x if i]
+        + [at(0, steps_z[n], 0, i) for n in direct for i in steps_x if i]
         + [at(j, 0, c, 0) for j, c in steps_q if j or c]
         + [before, after]
     )
     for partner in partners:
         pl.semaphore_signal(barrier, inc=1, device_id=partner, device_id_type=MESH)
+    for load in indices[2:]:
+        load.start()
 
     def rest_of(o):
         return slice(kinds * MAIN + o * rest_pad, kinds * MAIN + o * rest_pad + rest)
@@ -153,26 +187,29 @@
     m2m_p[:, kinds * MAIN :] = jnp.zeros((k, kinds * rest_pad), BF16)
     m2l_p[:, kinds * MAIN :] = jnp.zeros((k, kinds * rest_pad), BF16)
 
+    indices[0].wait()
+    indices[1].wait()
     cell = (
         lax.broadcasted_iota(I32, pa_ref.shape, 0) * LANES
         + lax.broadcasted_iota(I32, pa_ref.shape, 1)
     )
     code_a = oa_ref[...] * cells_b + pa_ref[...] - device * cells_b
-    code_a = jnp.where(cell < count_ref[...], code_a, -1)
+    code_a = jnp.where(cell < count_ref[0], code_a, -1)
     slot = lax.broadcasted_iota(I32, (8 * cells_b, LANES), 0)
     for r in range(cells_a // LANES):
         one_hot_a[:, r * LANES : (r + 1) * LANES] = (slot == code_a[r : r + 1, :]).astype(F32).astype(BF16)
 
-    loads[0].wait()
-    loads[1].wait()
+    for load in loads[0:2] + indices[2:]:
+        load.wait()
+    loads[2].start()
     separate(m2m_in, m2m_v, m2m_p)
-    for o in range(8):
-        m2m_t[o] = m2m_v[o].T
     for o in range(0, 8, 2):
         pair = dot(leaf_ref[...], one_hot_a[o * cells_b : (o + 2) * cells_b, :], (1, 1)).astype(BF16)
         put(o, pair[:, :cells_b])
         put(o + 1, pair[:, cells_b:])
-    mult_b = dot(m2m_p[...], stack[:, :cells_b]).astype(BF16)
+        m2m_t[o] = m2m_v[o].T
+        m2m_t[o + 1] = m2m_v[o + 1].T
+    mult_b = stacked_dot(m2m_p, stack[:, :cells_b]).astype(BF16)
     window[:, cells_b : 2 * cells_b] = jnp.zeros((window.shape[0], cells_b), BF16)
     window[0:k, cells_b : 2 * cells_b] = mult_b
 
@@ -215,20 +252,20 @@
 
     pl.semaphore_wait(barrier, len(partners))
 
-    sent_z = {}
-    for n, j in enumerate(steps_z):
-        if j:
-            sent_z[n] = send(part(gathered, 0), part(gathered, n * nx), sems_z, n - 1, at(0, j, 0, 0))
-    sent_x = {}
-
-    def spread(n):
+    sent_z, sent_x = {}, {}
+
+    def along_x(n, source, dz):
         for i in steps_x:
             if i:
                 sent_x[n, i] = send(
-                    part(gathered, n * nx), part(gathered, n * nx + i), sems_x, n * (nx - 1) + i - 1, at(0, 0, 0, i)
+                    part(gathered, source), part(gathered, n * nx + i), sems_x, n * (nx - 1) + i - 1, at(0, dz, 0, i)
                 )
 
-    spread(0)
+    for n in reversed(range(1, nz)):
+        sent_z[n] = send(part(gathered, 0), part(gathered, n * nx), sems_z, n - 1, at(0, steps_z[n], 0, 0))
+        if n in direct:
+            along_x(n, 0, steps_z[n])
+    along_x(0, 0, 0)
     sent_heads = {}
     for n, (j, c) in enumerate(steps_q):
         if n:
@@ -257,8 +294,9 @@
     separate(m2l_in, None, m2l_p)
 
     for n in range(1, nz):
-        sent_z[n].wait_recv()
-        spread(n)
+        if n not in direct:
+            sent_z[n].wait_recv()
+            along_x(n, n * nx, 0)
 
     mine = window.at[:, cells_b : 2 * cells_b]
     near_sems = (near_send, near_recv)
@@ -285,6 +323,8 @@
     chunk = min(LANES, half)
     for first in range(0, sources, chunk):
         for n in range(first // cells_c // nx, (first + chunk) // cells_c // nx):
+            if n in direct:
+                sent_z[n].wait_recv()
             for i in steps_x:
                 if i:
                     sent_x[n, i].wait_recv()
@@ -304,7 +344,7 @@
     for o in range(kinds):
         lanes = slice(o * targets, (o + 1) * targets)
         put(o, (early[:, lanes] + dot(turned[0:k, half:], count_t[half:, lanes])).astype(BF16))
-    partial = dot(m2l_p[...], stack[:, 0:targets])
+    partial = stacked_dot(m2l_p, stack[:, 0:targets])
     pad_v[0:k, 0:targets] = partial
     shares[...] = pad_v[:, 0:targets].T.astype(BF16)
 
@@ -319,7 +359,7 @@
         pair = dot(window[0:k, :], count_b[:, o * cells_b : (o + 2) * cells_b]).astype(BF16)
         put(o, pair[:, :cells_b])
         put(o + 1, pair[:, cells_b:])
-    near = dot(m2l_p[...], stack[:, 0:cells_b])
+    near = stacked_dot(m2l_p, stack[:, 0:cells_b])
     pad_v[0:k, 0:cells_b] = near
     near_t[...] = pad_v[:, 0:cells_b].T
     one_hot_bt = one_hot_b.T.astype(BF16)
@@ -382,6 +422,7 @@
     wide = max(cells_b, targets)
     stacked = kinds * (MAIN + -(-(k - MAIN) // 16) * 16)
     vmem = pl.BlockSpec(memory_space=pltpu.VMEM)
+    smem = pl.BlockSpec(memory_space=pltpu.SMEM)
     hbm = pl.BlockSpec(memory_space=pl.ANY)
 
     def here(array):
@@ -393,9 +434,19 @@
     fine = pl.pallas_call(
         functools.partial(kernel, dims),
         out_shape=pltpu.VMEM((k, cells_a), BF16),
-        in_specs=[hbm] + [vmem] * 11 + [hbm, hbm],
+        in_specs=[hbm, smem] + [hbm] * 10 + [hbm, hbm],
         out_specs=vmem,
         scratch_shapes=[
+            pltpu.VMEM((cells_a // LANES, LANES), I32),
+            pltpu.VMEM((cells_a // LANES, LANES), I32),
+            pltpu.VMEM((1, cells_b), I32),
+            pltpu.VMEM((1, cells_b), I32),
+            pltpu.VMEM((1, cells_c), I32),
+            pltpu.VMEM((1, cells_c), I32),
+            pltpu.VMEM(list_b_src.shape[::-1], I32),
+            pltpu.VMEM(list_b_src.shape[::-1], I32),
+            pltpu.VMEM(list_t_src.shape[::-1], I32),
+            pltpu.VMEM(list_t_src.shape[::-1], I32),
             pltpu.VMEM((k, cells_a), BF16),
             pltpu.VMEM((k, 8, k), BF16),
             pltpu.VMEM((k, kinds, k), BF16),
@@ -419,7 +470,7 @@
             pltpu.VMEM((targets, kp), BF16),
             pltpu.VMEM((8 * cells_c, k), F32),
             pltpu.VMEM((8 * cells_b, k), BF16),
-            pltpu.SemaphoreType.DMA((3,)),
+            pltpu.SemaphoreType.DMA((13,)),
             pltpu.SemaphoreType.DMA((2,)),
             pltpu.SemaphoreType.DMA((2,)),
             pair(nz - 1),
@@ -432,7 +483,7 @@
         ),
     )(
         here(leaf_mult),
-        fine_count.reshape(1, 1),
+        fine_count,
         here(parent_a.reshape(-1, LANES)),
         here(octant_a.reshape(-1, LANES)),
         here(parent_b.reshape(1, -1)),

time: 43.3 us -> 42 us (0.970)
  Pallas kernels: 41.7 us -> 40.3 us
    pallas_call x1, Pallas kernels: 41.7 us -> 40.3 us  [body(): pl.pallas_call(functools.partial(kernel, dims), out_shape=pltpu.VMEM((k,...]
where the time goes in v6:
time: 42 us; the launch traced here: 41.8 us
  Pallas kernels  40.3 us (96%)
  local copies, waits for them, and re-layouts  0.82 us (2%)
  between operations  0.66 us (2%)
    pallas_call x1, Pallas kernels, body(): pl.pallas_call(functools.partial(kernel, dims), out_shape=pltpu.VMEM((k,...  40.3 us

profile of v6, /device:TPU:1, one launch (start us, length us, event | category | flops | bytes accessed | tf_op | source)
XLA Modules:
  0.0 41.8 jit_solution(13070443342841631631)
XLA Ops:
  0.7 40.3 %shard_map.136 = bf16[289,1024]{1,0:T(8,128)(2,1)S(1)} custom-call(bf16[289,1024]{1,0:T(8,128)(2,1)} %leaf_hbm.1, s32[1]{0:T(128)S(6)} %copy.17.count_ref, s32[8,128]{1,0:T(8,128)} %bitcast.18, s32[8,128]{1,0:T(8,128)} %bitcast.19, s32[1,128]{1,0:T(1,128)} %bitcast.20, s32[1,128]{1,0:T(1,128)} %bitcast.21, s32[1,16]{1,0:T(1,128)} %bitcast.22, ...), custom_call_target="tpu_custom_call" | custom-call | tf_op jit(solution)/shard_map/pallas_call | solution.py:434
  41.0 0.8 %copy.16 = bf16[289,1024]{1,0:T(8,128)(2,1)} copy(bf16[289,1024]{1,0:T(8,128)(2,1)S(1)} %shard_map.136) | data formatting | bytes 1183744

commit v7 on v6

--- a/solution.py
+++ b/solution.py
@@ -116,7 +116,7 @@
         return (d // nx, lax.rem(d, nx))
 
     steps_z = sorted(range(nz), key=lambda i: (min(i, nz - i), i))
-    steps_x = range(nx)
+    steps_x = sorted(range(nx), key=lambda i: (-min(i, nx - i), i))
     direct = [n for n, j in enumerate(steps_z) if min(j, nz - j) == 1]
     steps_q = sorted(
         [(i, c) for i in range(ny) for c in range(CORES)], key=lambda s: (min(s[0], ny - s[0]), s)
@@ -266,8 +266,9 @@
         if n in direct:
             along_x(n, 0, steps_z[n])
     along_x(0, 0, 0)
+    far_first = list(reversed(list(enumerate(steps_q))))
     sent_heads = {}
-    for n, (j, c) in enumerate(steps_q):
+    for n, (j, c) in far_first:
         if n:
             sent_heads[n] = send(part(heads, 0), part(heads, n), sems_h, n - 1, at(j, 0, c, 0))
     def count(place, wanted, kind, store):
@@ -349,7 +350,7 @@
     shares[...] = pad_v[:, 0:targets].T.astype(BF16)
 
     sent_q = {}
-    for n, (j, c) in enumerate(steps_q):
+    for n, (j, c) in far_first:
         if n:
             sent_q[n] = send(part(shares, n), part(arrived, n), sems_q, n - 1, at(-j, 0, -c, 0))
 

time: 42 us -> 40.2 us (0.957)
  Pallas kernels: 40.3 us -> 38.6 us
    pallas_call x1, Pallas kernels: 40.3 us -> 38.6 us  [body(): pl.pallas_call(functools.partial(kernel, dims), out_shape=pltpu.VMEM((k,...]
where the time goes in v7:
time: 40.2 us; the launch traced here: 40.1 us
  Pallas kernels  38.6 us (96%)
  local copies, waits for them, and re-layouts  0.82 us (2%)
  between operations  0.66 us (2%)
    pallas_call x1, Pallas kernels, body(): pl.pallas_call(functools.partial(kernel, dims), out_shape=pltpu.VMEM((k,...  38.6 us
    unnamed x1, local copies, waits for them, and re-layouts  0.82 us

profile of v7, /device:TPU:1, one launch (start us, length us, event | category | flops | bytes accessed | tf_op | source)
XLA Modules:
  0.0 40.1 jit_solution(7018959072211077940)
XLA Ops:
  0.7 38.6 %shard_map.136 = bf16[289,1024]{1,0:T(8,128)(2,1)S(1)} custom-call(bf16[289,1024]{1,0:T(8,128)(2,1)} %leaf_hbm.1, s32[1]{0:T(128)S(6)} %copy.17.count_ref, s32[8,128]{1,0:T(8,128)} %bitcast.18, s32[8,128]{1,0:T(8,128)} %bitcast.19, s32[1,128]{1,0:T(1,128)} %bitcast.20, s32[1,128]{1,0:T(1,128)} %bitcast.21, s32[1,16]{1,0:T(1,128)} %bitcast.22, ...), custom_call_target="tpu_custom_call" | custom-call | tf_op jit(solution)/shard_map/pallas_call | solution.py:435
  39.2 0.8 %copy.16 = bf16[289,1024]{1,0:T(8,128)(2,1)} copy(bf16[289,1024]{1,0:T(8,128)(2,1)S(1)} %shard_map.136) | data formatting | bytes 1183744

commit v8 on v7

--- a/solution.py
+++ b/solution.py
@@ -149,10 +149,10 @@
 
     barrier = pltpu.get_barrier_semaphore()
     partners = (
-        [at(0, j, 0, 0) for j in steps_z if j]
+        [at(0, j, 0, 0) for j in reversed(steps_z) if j]
         + [at(0, 0, 0, i) for i in steps_x if i]
         + [at(0, steps_z[n], 0, i) for n in direct for i in steps_x if i]
-        + [at(j, 0, c, 0) for j, c in steps_q if j or c]
+        + [at(j, 0, c, 0) for j, c in reversed(steps_q) if j or c]
         + [before, after]
     )
     for partner in partners:

time: 40.2 us -> 40 us (level)
  no operation moved by 1% of the time
where the time goes in v8:
time: 40 us; the launch traced here: 39.9 us
  Pallas kernels  38.4 us (96%)
  local copies, waits for them, and re-layouts  0.82 us (2%)
  between operations  0.66 us (2%)
    pallas_call x1, Pallas kernels, body(): pl.pallas_call(functools.partial(kernel, dims), out_shape=pltpu.VMEM((k,...  38.4 us
    unnamed x1, local copies, waits for them, and re-layouts  0.82 us

profile of v8, /device:TPU:1, one launch (start us, length us, event | category | flops | bytes accessed | tf_op | source)
XLA Modules:
  0.0 39.9 jit_solution(13464381615822113110)
XLA Ops:
  0.7 38.4 %shard_map.136 = bf16[289,1024]{1,0:T(8,128)(2,1)S(1)} custom-call(bf16[289,1024]{1,0:T(8,128)(2,1)} %leaf_hbm.1, s32[1]{0:T(128)S(6)} %copy.17.count_ref, s32[8,128]{1,0:T(8,128)} %bitcast.18, s32[8,128]{1,0:T(8,128)} %bitcast.19, s32[1,128]{1,0:T(1,128)} %bitcast.20, s32[1,128]{1,0:T(1,128)} %bitcast.21, s32[1,16]{1,0:T(1,128)} %bitcast.22, ...), custom_call_target="tpu_custom_call" | custom-call | tf_op jit(solution)/shard_map/pallas_call | solution.py:435
  39.1 0.8 %copy.16 = bf16[289,1024]{1,0:T(8,128)(2,1)} copy(bf16[289,1024]{1,0:T(8,128)(2,1)S(1)} %shard_map.136) | data formatting | bytes 1183744
